TPU v7x, 32 devices: a whole 2x2x4 slice. The times are simulated.
32 devices in a mesh: segment: 2 (over core), ctx: 8 (over z, x), tp: 2 (over y).
Axes of the slice: x: 2, y: 2, z: 4, core: 2. Of those that a mesh axis runs over, the one named last changes fastest.
Arguments:
- queries: bfloat16 [1024, 32, 128], P('ctx', 'tp'), may hold values from -14 to 14
- keys: bfloat16 [1024, 8, 128], P('ctx', 'tp'), may hold values from -10 to 10
- values: bfloat16 [1024, 8, 128], P('ctx', 'tp'), may hold values from -6 to 6
- layer_in: bfloat16 [1024, 4096], P('ctx', 'tp'), may hold values from -6 to 6
- w_bc: bfloat16 [1, 4096, 1024], P(None, 'tp'), may hold values from -0.09375 to 0.09375
- w_dt: bfloat16 [1, 4096, 64], P(None, 'tp'), may hold values from -0.09375 to 0.09375
- dt_bias: float32 [1, 64], P(None, 'tp'), may hold values from -1 to 1
- decay_rate: float32 [1, 64], P(None, 'tp'), may hold values from 9.765625e-05 to 0.06
- skip_gain: float32 [1, 64], P(None, 'tp'), may hold values from 0.5 to 2
- out_gain: float32 [1, 64, 64], P(None, 'tp'), may hold values from 0.5 to 1.5
Outputs:
- section_out: bfloat16 [2, 1024, 4096], P('segment', 'ctx', 'tp')
All inputs are finite; a program needn't handle non-finite values.
Results may differ from a plain program's by a relative error of at most 0.002.
Values may be sent and summed in bfloat16 or wider, within the bound.
A program may use at most 256 MiB of HBM per device.

v0:
```python
import math

import jax
import jax.numpy as jnp
from jax import lax
from jax.sharding import PartitionSpec as P

GROUPS = 4
STATE = 128


EPSILON = 1e-05


def prefix(part, axis, combine, identity):
    place = lax.axis_index(axis)
    gathered = jax.tree.map(lambda a: lax.all_gather(a, axis), part)
    state = jax.tree.map(lambda a, e: jnp.zeros_like(a) + jnp.asarray(e, a.dtype), part, identity)

    def one(turn, state):
        return combine(
            state, jax.tree.map(lambda a: lax.dynamic_index_in_dim(a, turn, 0, False), gathered)
        )

    return lax.fori_loop(0, place, one, state)


def swapped(value, axis, distance):
    mask = 2**distance
    pairs = [(source, source ^ mask) for source in range(lax.axis_size(axis))]
    return lax.ppermute(value, axis, pairs)


def span_terms(normed, b_rows, c_rows, step_sizes, rate_row, skip_row):
    count_rows, head_count, head_width = normed.shape
    group_count = b_rows.shape[1]
    per_group = head_count // group_count
    state_root = math.sqrt(b_rows.shape[2])
    log_decay = jnp.cumsum(-step_sizes * rate_row[None, :], axis=0)
    lower_mask = jnp.arange(count_rows)[:, None] >= jnp.arange(count_rows)[None, :]
    intersection = (
        jnp.einsum("tgn,sgn->gts", c_rows, b_rows, precision=lax.Precision.HIGHEST) / state_root
    )
    log_gaps = log_decay.T[:, :, None] - log_decay.T[:, None, :]
    decays = jnp.where(lower_mask[None], jnp.exp(jnp.where(lower_mask[None], log_gaps, 0.0)), 0.0)
    mixing = (
        decays.reshape(group_count, per_group, count_rows, count_rows)
        * intersection[:, None]
        * step_sizes.T.reshape(group_count, per_group, 1, count_rows)
    )
    grouped = normed.reshape(count_rows, group_count, per_group, head_width)
    local_part = jnp.einsum(
        "gkts,sgkp->tgkp", mixing, grouped, precision=lax.Precision.HIGHEST
    ).reshape(count_rows, head_count, head_width)
    tail_weight = jnp.exp(log_decay[-1][None, :] - log_decay) * step_sizes
    weighted = (normed * tail_weight[:, :, None]).reshape(
        count_rows, group_count, per_group, head_width
    )
    ending = jnp.einsum(
        "sgkp,sgn->gkpn", weighted, b_rows, precision=lax.Precision.HIGHEST
    ).reshape(head_count, head_width, b_rows.shape[2])
    return (
        log_decay,
        local_part + skip_row[None, :, None] * normed,
        ending,
        jnp.exp(log_decay[-1]),
    )


def span_inflow(log_decay, c_rows, state_in):
    count_rows, group_count, state_n = c_rows.shape
    head_count, head_width = (state_in.shape[0], state_in.shape[1])
    per_group = head_count // group_count
    state_root = math.sqrt(state_n)
    inflow = jnp.einsum(
        "tgn,gkpn->tgkp",
        c_rows,
        state_in.reshape(group_count, per_group, head_width, state_n),
        precision=lax.Precision.HIGHEST,
    )
    return (
        jnp.exp(log_decay)[:, :, None]
        * inflow.reshape(count_rows, head_count, head_width)
        / state_root
    )


def merge_states(earlier, later):
    return (earlier[0] * later[0], later[0][:, None, None] * earlier[1] + later[1])


def body(queries, keys, values, layer_in, w_bc, w_dt, dt_bias, decay_rate, skip_gain, out_gain):
    segment_index = lax.axis_index("segment")
    attention_on = segment_index == 0
    state_on = jnp.logical_not(attention_on)
    row_count, q_heads, head_width = queries.shape
    kv_heads = keys.shape[1]
    group_size = q_heads // kv_heads
    score_scale = 1.0 / math.sqrt(head_width)
    first_row = lax.axis_index("ctx") * row_count
    last_row = first_row + row_count - 1
    query_place = first_row + jnp.arange(row_count, dtype=jnp.int32)
    grouped = queries.reshape(row_count, kv_heads, group_size, head_width).transpose(1, 2, 0, 3)

    def add_block(carried, key_block, value_block, key_start):
        row_top, row_total, row_sum = carried
        scores = (
            jnp.einsum("kgqd,skd->kgqs", grouped, key_block, preferred_element_type=jnp.float32)
            * score_scale
        )
        key_place = key_start + jnp.arange(key_block.shape[0], dtype=jnp.int32)
        allowed = (query_place[:, None] >= key_place[None, :])[None, None]
        masked = jnp.where(allowed, scores, -1e30)
        new_top = jnp.maximum(row_top, jnp.max(masked, axis=3))
        raw_weight = jnp.where(allowed, jnp.exp(masked - new_top[..., None]), 0.0)
        factor = jnp.exp(row_top - new_top)
        new_total = row_total * factor + jnp.sum(raw_weight, axis=3)
        block_sum = jnp.einsum(
            "kgqs,skd->kgqd",
            raw_weight.astype(jnp.bfloat16),
            value_block,
            preferred_element_type=jnp.float32,
        )
        return (new_top, new_total, row_sum * factor[..., None] + block_sum)

    initial = (
        jnp.full((kv_heads, group_size, row_count), -1e30, jnp.float32),
        jnp.zeros((kv_heads, group_size, row_count), jnp.float32),
        jnp.zeros((kv_heads, group_size, row_count, head_width), jnp.float32),
    )
    piece_start = jnp.int32(0)
    key_piece = lax.all_gather(keys, "ctx", axis=0, tiled=True)
    value_piece = lax.all_gather(values, "ctx", axis=0, tiled=True)
    key_count = key_piece.shape[0]
    block_size = math.gcd(key_count, 1024)

    def run_all(inner_state):
        if key_count == block_size:
            return add_block(inner_state, key_piece, value_piece, piece_start)

        def one_step(block_index, loop_state):
            block_start = block_index * block_size
            key_block = lax.dynamic_slice_in_dim(key_piece, block_start, block_size, 0)
            value_block = lax.dynamic_slice_in_dim(value_piece, block_start, block_size, 0)
            return add_block(loop_state, key_block, value_block, piece_start + block_start)

        return lax.fori_loop(0, key_count // block_size, one_step, inner_state)

    wanted = jnp.logical_and(attention_on, piece_start <= last_row)
    row_top, row_total, row_sum = lax.cond(wanted, run_all, lambda kept_state: kept_state, initial)
    safe_total = jnp.where(attention_on, row_total, 1.0)
    mixed_out = row_sum / safe_total[..., None]
    attended = (
        mixed_out.transpose(2, 0, 1, 3)
        .reshape(row_count, q_heads * head_width)
        .astype(jnp.bfloat16)
    )
    current = layer_in
    channel_count = current.shape[1]
    heads_dev = dt_bias.shape[1]
    state_width = channel_count // heads_dev
    groups_dev = GROUPS // lax.axis_size("tp")
    wide_rows = current.astype(jnp.float32)
    part_bc = jnp.dot(current, w_bc[0], preferred_element_type=jnp.float32)
    part_dt = jnp.dot(current, w_dt[0], preferred_element_type=jnp.float32)
    part_sq = jnp.sum(wide_rows * wide_rows, axis=1)
    sum_bc, sum_dt, sum_sq = lax.psum((part_bc, part_dt, part_sq), "tp")
    inv_rms = lax.rsqrt(sum_sq / (channel_count * lax.axis_size("tp")) + EPSILON)
    normed = (wide_rows * inv_rms[:, None]).reshape(row_count, heads_dev, state_width)
    half_cols = GROUPS * STATE
    b_all = sum_bc[:, :half_cols].reshape(row_count, GROUPS, STATE)
    c_all = sum_bc[:, half_cols:].reshape(row_count, GROUPS, STATE)
    group_start = lax.axis_index("tp") * groups_dev
    b_rows = lax.dynamic_slice_in_dim(b_all, group_start, groups_dev, 1) * inv_rms[:, None, None]
    c_rows = lax.dynamic_slice_in_dim(c_all, group_start, groups_dev, 1) * inv_rms[:, None, None]
    own_dt = lax.dynamic_slice_in_dim(sum_dt, lax.axis_index("tp") * heads_dev, heads_dev, 1)
    step_sizes = jax.nn.softplus(own_dt * inv_rms[:, None] + dt_bias[0][None, :])

    def compute_terms(given):
        return span_terms(given[0], given[1], given[2], given[3], decay_rate[0], skip_gain[0])

    def empty_terms(given):
        return (
            jnp.zeros((row_count, heads_dev), jnp.float32),
            jnp.zeros((row_count, heads_dev, state_width), jnp.float32),
            jnp.zeros((heads_dev, state_width, STATE), jnp.float32),
            jnp.zeros((heads_dev,), jnp.float32),
        )

    log_decay, local_part, ending, span_decay = lax.cond(
        state_on, compute_terms, empty_terms, (normed, b_rows, c_rows, step_sizes)
    )
    decay_in, state_in = prefix(
        (span_decay, ending),
        "ctx",
        merge_states,
        (jnp.ones_like(span_decay), jnp.zeros_like(ending)),
    )
    mixed_out = local_part + span_inflow(log_decay, c_rows, state_in)
    power = jnp.mean(mixed_out * mixed_out, axis=2, keepdims=True)
    result = wide_rows.reshape(row_count, heads_dev, state_width) + out_gain[0][
        None
    ] * mixed_out * lax.rsqrt(power + EPSILON)
    current = result.reshape(row_count, channel_count).astype(jnp.bfloat16)
    result = jnp.where(attention_on, attended, current)
    incoming = swapped(result, "segment", 0)
    return incoming[None]


def solution(mesh):
    in_specs = (
        P("ctx", "tp", None),
        P("ctx", "tp", None),
        P("ctx", "tp", None),
        P("ctx", "tp"),
        P(None, "tp", None),
        P(None, "tp", None),
        P(None, "tp"),
        P(None, "tp"),
        P(None, "tp"),
        P(None, "tp", None),
    )
    out_specs = P("segment", "ctx", "tp")
    return jax.shard_map(body, mesh=mesh, in_specs=in_specs, out_specs=out_specs, check_vma=False)
```

profile of v0, /device:TPU:24, one launch (start us, length us, event | category | flops | bytes accessed | tf_op | source)
XLA Modules:
  0.0 246.6 jit_solution(6221878854511124643)
XLA Ops:
  7.4 0.0 all-reduce.4.cloned.1.call-start
  7.4 3.9 %fusion.39 = f32[128,1024]{1,0:T(8,128)} fusion(bf16[128,2048]{1,0:T(8,128)(2,1)} %param.19, bf16[1,2048,1024]{2,1,0:T(8,128)(2,1)} %param.20), kind=kOutput, calls=%fused_computation.53 | convolution fusion | flops 536870912 | bytes 5242880 | tf_op jit(solution)/shard_map/dot_general | solution.py:164
  11.3 0.0 all-reduce.4.cloned.1.call-update
  11.4 0.0 all-gather.6.cloned.1.call-start
  11.4 1.6 copy.50
  13.0 0.0 all-gather.6.cloned.1.call-update
  13.0 0.0 all-gather.8.cloned.1.call-start
  13.1 1.6 copy.51
  14.7 0.0 all-gather.8.cloned.1.call-update
  14.7 0.0 all-gather.10.cloned.1.call-start
  14.7 1.3 copy.53
  16.1 0.1 convert_element_type.31
  16.1 0.3 multiply_reduce_fusion.1
  16.4 0.3 fusion.44
  16.7 9.3 %all-reduce.1 = (f32[128,64]{0,1:T(8,128)S(1)}, f32[128]{0:T(128)S(1)}) all-reduce(f32[128,64]{0,1:T(8,128)S(1)} %fusion.44, f32[128]{0:T(128)S(1)} %multiply_reduce_fusion.1), channel_id=1, replica_groups=mesh['segment'=2,'ctx'=8,'tp'=2] {'tp'}, use_global_device_ids=true, to_apply=%region_4.5 | all-reduce | flops 8320 | bytes 66560 | tf_op jit(solution)/shard_map/psum | solution.py:167
  26.1 15.9 %all-reduce.4.cloned.1.call-done = f32[128,1024]{1,0:T(8,128)} async-done(((f32[128,1024]{1,0:T(8,128)}), f32[128,1024]{1,0:T(8,128)}) %all-reduce.4.cloned.1.call-update) | async-done | bytes 524304 | tf_op jit(solution)/shard_map/psum | solution.py:167
  42.0 1.0 slice.20
  42.9 0.1 reshape.121
  43.0 0.1 constant_dynamic-slice_fusion
  43.1 0.1 copy_multiply_fusion
  43.2 0.7 mul.208
  43.8 0.0 copy-done.5
  43.9 1.9 conditional.3
  43.9 0.1 broadcast.91
  44.0 1.1 broadcast.92
  45.1 0.6 broadcast.90
  45.7 0.0 all-gather.10.cloned.1.call-update
  45.7 2.0 copy.49
  47.7 1.3 dynamic-slice
  49.7 0.2 dynamic-update-slice
  50.0 16.8 %all-reduce = f32[256]{0:T(256)S(1)} all-reduce(f32[256]{0:T(256)S(1)} %dynamic-update-slice), channel_id=2, replica_groups=mesh['segment'=2,'ctx'=8,'tp'=2] {'ctx'}, use_global_device_ids=true, to_apply=%add | all-reduce | flops 256 | bytes 2048
  66.7 0.7 reshape.124
  67.4 0.9 exp.40
  68.3 0.1 copy.58
  68.3 27.1 %all-gather.8.cloned.1.call-done = bf16[1024,4,128]{2,0,1:T(8,128)(2,1)} async-done(((bf16[128,4,128]{2,0,1:T(8,128)(2,1)}), bf16[1024,4,128]{2,0,1:T(8,128)(2,1)}) %all-gather.8.cloned.1.call-update) | async-done | bytes 1048592 | tf_op jit(solution)/shard_map/all_gather | solution.py:133
  95.5 8.8 %conditional.2 = (f32[4,4,128]{2,1,0:T(4,128)S(1)}, f32[4,4,128,128]{3,2,1,0:T(8,128)S(1)}) conditional(s32[]{:T(128)} %convert_element_type.27, () %tuple.39, (s32[]{:T(128)}, s32[128]{0:T(128)S(1)}, bf16[4,4,128,128]{3,2,1,0:T(8,128)(2,1)}, bf16[1024,4,128]{2,0,1:T(8,128)(2,1)}, bf16[1024,4,128]{2,0,1:T(8,128)(2,1)}) %tuple.73), branch_computations={%region_0.0_spmd, %region_1.4_spmd} | conditional | flops 1101404288 | bytes 33646128 | solution.py:150
  95.5 0.1 iota_compare_fusion
  95.6 3.1 %fusion = (f32[4,4,128]{2,1,0:T(4,128)S(1)}, f32[4,4,128,1024]{3,2,1,0:T(8,128)S(1)}) fusion(pred[128,1024]{1,0:T(8,128)(4,1)S(1)} %iota_compare_fusion, bf16[4,4,128,128]{3,2,1,0:T(8,128)(2,1)} %get-tuple-element.203, bf16[1024,4,128]{2,0,1:T(8,128)(2,1)} %get-tuple-element.204), kind=kOutput, calls=%fused_computation.2 | convolution fusion | flops 543160320 | bytes 10100736 | tf_op jit(solution)/shard_map/cond/branch_1_fun/kgqd,skd->kgqs/dot_general | solution.py:108
  98.7 2.7 %fusion.2 = f32[4,4,128]{2,1,0:T(4,128)S(1)} fusion(f32[4,4,128,1024]{3,2,1,0:T(8,128)S(1)} %get-tuple-element.292, f32[4,4,128]{2,1,0:T(4,128)S(1)} %broadcast_maximum_fusion, pred[128,1024]{1,0:T(8,128)(4,1)S(1)} %iota_compare_fusion), kind=kLoop, calls=%fused_computation.4 | loop fusion | flops 10483712 | bytes 8536064 | tf_op jit(solution)/shard_map/cond/branch_1_fun/reduce_sum | solution.py:117
  101.4 2.9 %fusion.6 = f32[4,4,128,128]{3,2,1,0:T(8,128)S(1)} fusion(f32[4,4,128,1024]{3,2,1,0:T(8,128)S(1)} %get-tuple-element.292, f32[4,4,128]{2,1,0:T(4,128)S(1)} %broadcast_maximum_fusion, pred[128,1024]{1,0:T(8,128)(4,1)S(1)} %iota_compare_fusion, bf16[1024,4,128]{2,0,1:T(8,128)(2,1)S(1)} %copy-done.7, f32[4,4,128]{2,1,0:T(4,128)S(1)} %get-tuple-element.289), kind=kOutput, calls=%fused_computation.7 | convolution fusion | flops 547618816 | bytes 10633216 | tf_op jit(solution)/shard_map/cond/branch_1_fun/kgqs,skd->kgqd/dot_general | solution.py:118
  104.3 1.1 fusion.43
  105.5 2.2 copy.52
  107.6 112.6 %all-gather.10.cloned.1.call-done = f32[256,64,128]{2,1,0:T(8,128)} async-done(((f32[32,64,128]{2,1,0:T(8,128)}), f32[256,64,128]{2,1,0:T(8,128)}) %all-gather.10.cloned.1.call-update) | async-done | bytes 8388624 | tf_op jit(solution)/shard_map/all_gather | solution.py:17
  220.3 0.1 broadcast.96
  220.4 13.0 %while.12 = (s32[]{:T(128)}, f32[32,64,128]{2,1,0:T(8,128)S(1)}, s32[]{:T(128)}, f32[8,32]{1,0:T(8,128)}, f32[8,32,64,128]{3,2,1,0:T(8,128)}, /*index=5*/s32[]{:T(128)}, s32[]{:T(128)}, s32[]{:T(128)}) while((s32[]{:T(128)}, f32[32,64,128]{2,1,0:T(8,128)S(1)}, s32[]{:T(128)}, f32[8,32]{1,0:T(8,128)}, f32[8,32,64,128]{3,2,1,0:T(8,128)}, ...), condition=%wide.region_12.13_spmd, body=%wide.region_11.12_spmd.sunk | while | flops 524293 | bytes 3146239 | solution.py:25
  220.4 0.7 dynamic-slice_bitcast_fusion.2
  221.1 1.4 bitcast_add_fusion.3
  222.6 0.7 dynamic-slice_bitcast_fusion.2
  223.3 1.4 bitcast_add_fusion.3
  224.7 0.7 dynamic-slice_bitcast_fusion.2
  225.4 1.4 bitcast_add_fusion.3
  226.9 0.7 dynamic-slice_bitcast_fusion.2
  227.6 1.4 bitcast_add_fusion.3
  229.1 0.7 dynamic-slice_bitcast_fusion.2
  229.8 1.4 bitcast_add_fusion.3
  231.2 0.7 dynamic-slice_bitcast_fusion.2
  231.9 1.4 bitcast_add_fusion.3
  233.4 1.0 fusion.46
  234.4 0.3 multiply_reduce_fusion
  234.7 1.1 add_convert_fusion
  235.9 0.1 bitcast_select_fusion
  236.0 0.1 collective-permute-start
  236.1 1.9 collective-permute-done
  238.0 1.0 copy.59
  (21 shorter events, 0.1 us)
Async XLA Ops:
  7.4 9.1 %copy-start = (bf16[1,2048,64]{1,2,0:T(8,128)(2,1)S(1)}, bf16[1,2048,64]{1,2,0:T(8,128)(2,1)}, u32[]{:S(2)}) copy-start(bf16[1,2048,64]{1,2,0:T(8,128)(2,1)} %param.21) | copy-start | bytes 786436
  7.4 9.1 %copy-start.1 = (bf16[128,2048]{1,0:T(8,128)(2,1)S(1)}, bf16[128,2048]{1,0:T(8,128)(2,1)}, u32[]{:S(2)}) copy-start(bf16[128,2048]{1,0:T(8,128)(2,1)} %param.19) | copy-start | bytes 1572868
  7.4 36.5 %copy-start.5 = (f32[1,32]{1,0:T(1,128)S(1)}, f32[1,32]{1,0:T(1,128)}, u32[]{:S(2)}) copy-start(f32[1,32]{1,0:T(1,128)} %param.22) | copy-start | bytes 388
  7.4 36.5 %copy-start.6 = (f32[1,32]{1,0:T(1,128)S(1)}, f32[1,32]{1,0:T(1,128)}, u32[]{:S(2)}) copy-start(f32[1,32]{1,0:T(1,128)} %param.23) | copy-start | bytes 388
  7.4 34.6 %all-reduce.4.cloned.1.call-start = ((), (), s32[]{:S(2)}) async-start(), calls=%async_computation.2 | async-start | bytes 1048576 | tf_op jit(solution)/shard_map/psum | solution.py:167
  11.4 57.0 %all-gather.6.cloned.1.call-start = ((), (), s32[]{:S(2)}) async-start(), calls=%async_computation | async-start | bytes 1179648 | tf_op jit(solution)/shard_map/all_gather | solution.py:132
  13.0 82.4 %all-gather.8.cloned.1.call-start = ((), (), s32[]{:S(2)}) async-start(), calls=%async_computation.1 | async-start | bytes 1179648 | tf_op jit(solution)/shard_map/all_gather | solution.py:133
  14.7 205.6 %all-gather.10.cloned.1.call-start = ((), (), s32[]{:S(2)}) async-start(), calls=%async_computation.3 | async-start | bytes 9437184 | tf_op jit(solution)/shard_map/all_gather | solution.py:17
  95.6 5.8 %copy-start.7 = (bf16[1024,4,128]{2,0,1:T(8,128)(2,1)S(1)}, bf16[1024,4,128]{2,0,1:T(8,128)(2,1)}, u32[]{:S(2)}) copy-start(bf16[1024,4,128]{2,0,1:T(8,128)(2,1)} %get-tuple-element.205) | copy-start | bytes 3145732 | tf_op jit(solution)/shard_map/cond
  233.4 2.5 %copy-start.2 = (bf16[128,4,4,128]{0,3,2,1:T(8,128)(2,1)S(1)}, bf16[128,4,4,128]{0,3,2,1:T(8,128)(2,1)}, u32[]{:S(2)}) copy-start(bf16[128,4,4,128]{0,3,2,1:T(8,128)(2,1)} %copy.52) | copy-start | bytes 1572868
  236.0 2.0 collective-permute-start
Sparse Core Ops, SparseCore 0:
  11.5 30.4 all-reduce.3
Sparse Core Ops, SparseCore 1:
  14.3 39.9 all-gather.5
  56.5 38.9 all-gather.7
  97.7 122.5 all-gather.9
where the time goes:
time: 249 us; the launch traced here: 247 us
  waiting for transfers between devices  158 us (63%)
  blocking collectives  26.1 us (10%)
  local copies, waits for them, and re-layouts  20.7 us (8%)
  between operations  15.9 us (6%)
  other arithmetic  14.6 us (6%)
  matrix products  11.2 us (4%)
    all_gather x1, waiting for transfers between devices, prefix(): gathered = jax.tree.map(lambda a: lax.all_gather(a, axis), part)  113 us
    all_gather x1, waiting for transfers between devices, body(): value_piece = lax.all_gather(values, 'ctx', axis=0, tiled=True)  27.1 us
    unnamed x1, blocking collectives  16.8 us
    psum x1, waiting for transfers between devices, body(): sum_bc, sum_dt, sum_sq = lax.psum((part_bc, part_dt, part_sq), 'tp')  15.9 us
    psum x1, blocking collectives, body(): sum_bc, sum_dt, sum_sq = lax.psum((part_bc, part_dt, part_sq), 'tp')  9.3 us
    add x6, other arithmetic, merge_states(): later[0][:, None, None] * earlier[1] + later[1]  8.63 us
    unnamed x17, local copies, waits for them, and re-layouts  8.02 us
  transfers between devices with their start and end apart: 5, of which 4 were waited for; matrix products, arithmetic and copies ran while one was open for 11% of the time, Pallas kernels for 0%

commit v1 on v0

v1 whole, which is shorter than its diff:
```python
import functools
import math

import jax
import jax.numpy as jnp
from jax import lax
from jax.experimental import pallas as pl
from jax.experimental.pallas import tpu as pltpu
from jax.sharding import PartitionSpec as P

MESH = pl.DeviceIdType.MESH
EPSILON = 1e-05
F32 = jnp.float32
BF16 = jnp.bfloat16

ROWS = 128
HEAD = 128
STATE = 128
SHEAD = 64
GHEADS = 16
GCOLS = GHEADS * SHEAD
GROUPS = 4
QH = 8
CHUNKS = 4
CCOLS = GCOLS // CHUNKS
MISC = 24
PACK = 2 * ROWS + MISC


def split(a):
    hi = a.astype(BF16)
    return hi, (a - hi.astype(F32)).astype(BF16)


def dot(a, b):
    return jnp.dot(a, b, preferred_element_type=F32)


def dot_t(a, b):
    return lax.dot_general(a, b, (((1,), (1,)), ((), ())), preferred_element_type=F32)


def dot3(a, b):
    return dot(a[0], b[0]) + (dot(a[0], b[1]) + dot(a[1], b[0]))


def dot3_t(a, b):
    return dot_t(a[0], b[0]) + (dot_t(a[0], b[1]) + dot_t(a[1], b[0]))


def lane_pair(left, right, shape):
    lane = lax.broadcasted_iota(jnp.int32, shape, 1)
    return jnp.where(lane < SHEAD, jnp.broadcast_to(left, shape), jnp.broadcast_to(right, shape))


def kernel(
    nz,
    q_hbm,
    kv_hbm,
    x_hbm,
    w_hbm,
    wdt_hbm,
    par_ref,
    row_ref,
    out_ref,
    qbuf,
    kvbuf,
    scores,
    xv,
    wv,
    wdtv,
    xg,
    psend,
    pbuf,
    tcols,
    rows_s,
    bt_s,
    c_s,
    cb_s,
    ending,
    s_in,
    s_out,
    local,
    stage,
    loc_sem,
    q_sem,
    kv_send,
    kv_recv,
    x_sem,
    p_send,
    p_recv,
    st_send,
    st_recv,
    o_send,
    o_recv,
):
    seg = lax.axis_index("segment")
    ctx = lax.axis_index("ctx")
    tp = lax.axis_index("tp")
    z = ctx // 2
    half = ctx % 2
    other = 1 - half
    pair = z * 2 + other
    barrier = pltpu.get_barrier_semaphore()
    my_rows = pl.ds(pl.multiple_of(half * ROWS, ROWS), ROWS)
    other_rows = pl.ds(pl.multiple_of(other * ROWS, ROWS), ROWS)
    my_cols = pl.ds(pl.multiple_of(half * GCOLS, GCOLS), GCOLS)
    other_cols = pl.ds(pl.multiple_of(other * GCOLS, GCOLS), GCOLS)

    def signal(s, c, t):
        pl.semaphore_signal(barrier, inc=1, device_id=(s, c, t), device_id_type=MESH)

    def remote(src, dst, send, recv, c, t):
        return pltpu.make_async_remote_copy(
            src_ref=src,
            dst_ref=dst,
            send_sem=send,
            recv_sem=recv,
            device_id=(seg, c, t),
            device_id_type=MESH,
        )

    @pl.when(seg == 1)
    def _attention():
        own_q = pltpu.make_async_copy(q_hbm.at[half], qbuf.at[:, my_rows, :], loc_sem.at[0])
        own_kv = pltpu.make_async_copy(kv_hbm.at[half], kvbuf.at[z, :, my_rows, :], loc_sem.at[1])
        own_q.start()
        own_kv.start()
        signal(1, pair, tp)

        def greet(zz, carry):
            signal(1, zz * 2, tp)
            signal(1, zz * 2 + 1, tp)
            return carry

        lax.fori_loop(0, z, greet, 0)
        pl.semaphore_wait(barrier, 1 + 2 * (nz - 1 - z))

        def kv_copy(part, c):
            return remote(
                kv_hbm.at[part], kvbuf.at[z, :, my_rows, :], kv_send.at[c], kv_recv.at[ctx], c, tp
            )

        def kv_arrival(c, src_z, src_rows):
            return remote(
                kv_hbm.at[half], kvbuf.at[src_z, :, src_rows, :], kv_send.at[c], kv_recv.at[c], c, tp
            )

        def q_copy(dst_rows):
            return remote(
                q_hbm.at[other], qbuf.at[:, dst_rows, :], q_sem.at[0], q_sem.at[1], pair, tp
            )

        def start_far(zz, carry):
            kv_copy(0, zz * 2).start()
            kv_copy(1, zz * 2 + 1).start()
            return carry

        lax.fori_loop(z + 1, nz, start_far, 0)
        kv_copy(other, pair).start()
        q_copy(my_rows).start()
        own_q.wait()
        own_kv.wait()
        q_copy(other_rows).wait_recv()
        kv_arrival(pair, z, other_rows).wait_recv()

        def arrive(zz, carry):
            kv_arrival(zz * 2, zz, pl.ds(0, ROWS)).wait_recv()
            kv_arrival(zz * 2 + 1, zz, pl.ds(ROWS, ROWS)).wait_recv()
            return carry

        lax.fori_loop(0, z, arrive, 0)
        scale = 1.0 / math.sqrt(HEAD)
        span = 2 * ROWS
        rows2 = 2 * span
        t_at = lax.broadcasted_iota(jnp.int32, (rows2, span), 0) % span
        s_at = lax.broadcasted_iota(jnp.int32, (rows2, span), 1)
        allowed = t_at >= s_at

        def two_heads(i, carry):
            kvh = i // 2
            q = qbuf[pl.ds(i * 2, 2)].reshape(rows2, HEAD)
            diag = dot_t(q, kvbuf[z, kvh]) * scale
            diag = jnp.where(allowed, diag, -1e30)

            def first(zz, top):
                s = dot_t(q, kvbuf[zz, kvh]) * scale
                scores[zz] = s
                return jnp.maximum(top, jnp.max(s, axis=1, keepdims=True))

            top = lax.fori_loop(0, z, first, jnp.max(diag, axis=1, keepdims=True))
            weight = jnp.exp(diag - top)
            total = jnp.sum(weight, axis=1, keepdims=True)
            acc = dot(weight.astype(BF16), kvbuf[z, kvh + 2])

            def second(zz, kept):
                total, acc = kept
                weight = jnp.exp(scores[zz] - top)
                return (
                    total + jnp.sum(weight, axis=1, keepdims=True),
                    acc + dot(weight.astype(BF16), kvbuf[zz, kvh + 2]),
                )

            total, acc = lax.fori_loop(0, z, second, (total, acc))
            done = (acc / total).astype(BF16)
            for k in range(2):
                cols = pl.ds(pl.multiple_of((i * 2 + k) * HEAD, HEAD), HEAD)
                stage[:, cols] = done[k * span : (k + 1) * span]
            return carry

        lax.fori_loop(0, QH // 2, two_heads, 0)

        def out_copy(cols):
            return remote(
                stage.at[other_rows, :], out_ref.at[:, cols], o_send.at[0], o_recv.at[0], pair, tp
            )

        out_copy(my_cols).start()
        out_ref[:, my_cols] = stage[my_rows, :]
        out_copy(my_cols).wait_send()
        out_copy(other_cols).wait_recv()

        def sent(zz, carry):
            kv_copy(0, zz * 2).wait_send()
            kv_copy(1, zz * 2 + 1).wait_send()
            return carry

        lax.fori_loop(z + 1, nz, sent, 0)
        kv_copy(other, pair).wait_send()
        q_copy(my_rows).wait_send()

    @pl.when(seg == 0)
    def _state():
        me4 = tp * 2 + half
        get_w = pltpu.make_async_copy(w_hbm, wv, loc_sem.at[0])
        get_x = pltpu.make_async_copy(x_hbm, xv, loc_sem.at[1])
        get_dt = pltpu.make_async_copy(wdt_hbm, wdtv, loc_sem.at[2])
        get_g = pltpu.make_async_copy(x_hbm.at[:, my_cols], xg.at[my_rows, :], loc_sem.at[3])
        get_x.start()
        get_w.start()
        get_dt.start()
        get_g.start()
        quad = ((z * 2 + half, 1 - tp), (pair, 1 - tp), (pair, tp))
        for c, t in quad:
            signal(0, c, t)

        @pl.when(z > 0)
        def _():
            signal(0, ctx - 2, tp)

        more = jnp.where(z < nz - 1, 1, 0)
        pl.semaphore_wait(barrier, 3 + more)

        def x_copy(dst_rows):
            return remote(
                x_hbm.at[:, other_cols], xg.at[dst_rows, :], x_sem.at[0], x_sem.at[1], pair, tp
            )

        x_copy(my_rows).start()
        get_x.wait()
        get_dt.wait()
        get_w.wait()
        x = xv[...]
        proj = dot(x, wv[...])
        dt_all = lax.dot_general(
            wdtv[...], x, (((0,), (1,)), ((), ())), preferred_element_type=F32
        )
        wide = x.astype(F32)
        sq_col = jnp.sum(wide * wide, axis=1, keepdims=True)
        sq_row = jnp.transpose(jnp.broadcast_to(sq_col, (ROWS, ROWS)))[0:8]
        for g in range(GROUPS):
            psend[g, 0:ROWS] = proj[:, g * STATE : (g + 1) * STATE]
            psend[g, ROWS : 2 * ROWS] = proj[:, (GROUPS + g) * STATE : (GROUPS + g + 1) * STATE]
            psend[g, 2 * ROWS : 2 * ROWS + GHEADS] = dt_all[g * GHEADS : (g + 1) * GHEADS]
            psend[g, 2 * ROWS + GHEADS : PACK] = sq_row

        def p_copy(k, slot):
            c, t = quad[k]
            to4 = t * 2 + c % 2
            return remote(
                psend.at[to4], pbuf.at[slot], p_send.at[k], p_recv.at[k], c, t
            )

        for k in range(3):
            p_copy(k, me4).start()
        pbuf[me4] = psend[me4]
        get_g.wait()
        x_copy(other_rows).wait_recv()
        for k in range(3):
            c, t = quad[k]
            p_copy(k, t * 2 + c % 2).wait_recv()

        span = 2 * ROWS
        r0 = pbuf[0] + pbuf[2]
        r1 = pbuf[1] + pbuf[3]
        b = jnp.concatenate([r0[0:ROWS], r1[0:ROWS]], axis=0)
        c_raw = jnp.concatenate([r0[ROWS : 2 * ROWS], r1[ROWS : 2 * ROWS]], axis=0)
        misc = jnp.concatenate([r0[2 * ROWS :], r1[2 * ROWS :]], axis=1)
        channels = 4 * GCOLS
        inv8 = lax.rsqrt(misc[GHEADS:MISC] / channels + EPSILON)
        inv = inv8[0:1]
        heads = pl.ds(pl.multiple_of(half * GHEADS, GHEADS), GHEADS)
        bias = par_ref[0, heads]
        rate = par_ref[1, heads]
        pre = misc[0:GHEADS] * inv + bias
        step = jnp.maximum(pre, 0.0) + jnp.log1p(jnp.exp(-jnp.abs(pre)))
        neg = -(step * rate)
        upto = (
            lax.broadcasted_iota(jnp.int32, (span, span), 0)
            <= lax.broadcasted_iota(jnp.int32, (span, span), 1)
        ).astype(F32).astype(BF16)
        n0 = neg.astype(BF16)
        rest = neg - n0.astype(F32)
        n1 = rest.astype(BF16)
        n2 = (rest - n1.astype(F32)).astype(BF16)
        log_decay = dot(n0, upto) + (dot(n1, upto) + dot(n2, upto))
        log_end = log_decay[:, span - 1 : span]
        u = step * inv
        root = math.sqrt(STATE)
        tall = jnp.concatenate(
            [
                log_decay,
                jnp.exp(log_end - log_decay) * u * inv,
                jnp.exp(log_decay) * inv / root,
                inv8,
                jnp.zeros((STATE - 3 * GHEADS - 8, span), F32),
            ],
            axis=0,
        )
        cols = jnp.transpose(tall)
        tcols[...] = cols
        rows_s[0] = log_decay
        rows_s[1] = u
        inv_col = cols[:, 3 * GHEADS : 3 * GHEADS + 1]
        bt_hi, bt_lo = split(jnp.transpose(b))
        c_hi, c_lo = split(c_raw)
        c_s[0] = c_hi
        c_s[1] = c_lo
        cb = dot3((c_hi, c_lo), (bt_hi, bt_lo)) * inv_col * inv / root
        lower = (
            lax.broadcasted_iota(jnp.int32, (span, span), 0)
            >= lax.broadcasted_iota(jnp.int32, (span, span), 1)
        )
        cb_s[...] = jnp.where(lower, cb, 0.0)

        def columns(base, j):
            parts = []
            for k in range(2):
                h = base + 4 * j + 2 * k
                parts.append(
                    lane_pair(cols[:, h : h + 1], cols[:, h + 1 : h + 2], (span, 2 * SHEAD))
                )
            return jnp.concatenate(parts, axis=1)

        def state_copy(j):
            return remote(
                s_out.at[j], s_in.at[j], st_send.at[j], st_recv.at[j],
                lax.rem(ctx + 2, 2 * nz), tp,
            )

        for j in range(CHUNKS):
            xc = xg[:, j * CCOLS : (j + 1) * CCOLS].astype(F32)
            e = dot3((bt_hi, bt_lo), split(xc * columns(GHEADS, j)))
            ending[j] = e

            @pl.when(z == 0)
            def _():
                s_out[j] = e
                s_in[j] = jnp.zeros_like(e)
                state_copy(j).start()

        for j in range(CHUNKS):
            for k in range(2):
                h = 4 * j + 2 * k
                xp = xg[:, h * SHEAD : (h + 2) * SHEAD]
                halves = []
                for d in range(2):
                    lrow = rows_s[0, h + d : h + d + 1]
                    urow = rows_s[1, h + d : h + d + 1]
                    lcol = tcols[:, h + d : h + d + 1]
                    top = (
                        jnp.exp(jnp.minimum(lcol[:ROWS] - lrow[:, :ROWS], 0.0))
                        * cb_s[:ROWS, :ROWS]
                        * urow[:, :ROWS]
                    )
                    low = jnp.exp(jnp.minimum(lcol[ROWS:] - lrow, 0.0)) * cb_s[ROWS:] * urow
                    t_hi, t_lo = split(top)
                    l_hi, l_lo = split(low)
                    halves.append(
                        (
                            dot(t_hi, xp[:ROWS]) + dot(t_lo, xp[:ROWS]),
                            dot(l_hi, xp) + dot(l_lo, xp),
                        )
                    )
                lane = lax.broadcasted_iota(jnp.int32, (ROWS, 2 * SHEAD), 1)
                at = slice(h * SHEAD, (h + 2) * SHEAD)
                local[0:ROWS, at] = jnp.where(lane < SHEAD, halves[0][0], halves[1][0])
                local[ROWS:span, at] = jnp.where(lane < SHEAD, halves[0][1], halves[1][1])

            @pl.when(z > 0)
            def _():
                state_copy(j).wait_recv()

                @pl.when(z < nz - 1)
                def _():
                    fade = []
                    for k in range(2):
                        h = 4 * j + 2 * k
                        last = tcols[span - 8 : span, 0:STATE][7:8]
                        fade.append(
                            lane_pair(
                                jnp.exp(last[:, h : h + 1]),
                                jnp.exp(last[:, h + 1 : h + 2]),
                                (1, 2 * SHEAD),
                            )
                        )
                    s_out[j] = s_in[j] * jnp.concatenate(fade, axis=1) + ending[j]
                    state_copy(j).start()

        block = (
            lax.broadcasted_iota(jnp.int32, (CCOLS, CCOLS), 0) // SHEAD
            == lax.broadcasted_iota(jnp.int32, (CCOLS, CCOLS), 1) // SHEAD
        ).astype(F32).astype(BF16)

        def out_copy(j, base):
            at = pl.ds(pl.multiple_of(base * GCOLS + j * CCOLS, CCOLS), CCOLS)
            return remote(
                stage.at[other_rows, pl.ds(j * CCOLS, CCOLS)],
                out_ref.at[:, at],
                o_send.at[j],
                o_recv.at[j],
                pair,
                tp,
            )

        for j in range(CHUNKS):
            at = slice(j * CCOLS, (j + 1) * CCOLS)
            xc = xg[:, at].astype(F32)
            inflow = dot3((c_s[0], c_s[1]), split(s_in[j]))
            gcols = pl.ds(pl.multiple_of(half * GCOLS + j * CCOLS, CCOLS), CCOLS)
            skip = row_ref[0:1, gcols]
            gain = row_ref[1:2, gcols]
            mixed = local[:, at] + inflow * columns(2 * GHEADS, j) + skip * (xc * inv_col)
            p_hi, p_lo = split(mixed * mixed)
            power = (dot(p_hi, block) + dot(p_lo, block)) / SHEAD
            stage[:, at] = (xc + gain * mixed * lax.rsqrt(power + EPSILON)).astype(BF16)
            out_copy(j, half).start()
            out_ref[:, gcols] = stage[my_rows, at]

        for j in range(CHUNKS):
            out_copy(j, half).wait_send()
            out_copy(j, other).wait_recv()

            @pl.when(z < nz - 1)
            def _():
                state_copy(j).wait_send()

        for k in range(3):
            p_copy(k, me4).wait_send()
        x_copy(my_rows).wait_send()


def body(queries, keys, values, layer_in, w_bc, w_dt, dt_bias, decay_rate, skip_gain, out_gain):
    nctx = lax.axis_size("ctx")
    nz = nctx // 2
    span = 2 * ROWS
    q = queries.transpose(1, 0, 2).reshape(2, QH, ROWS, HEAD)
    kv = jnp.stack([keys.reshape(ROWS, 2, 2, HEAD), values.reshape(ROWS, 2, 2, HEAD)], axis=0)
    kv = kv.transpose(2, 0, 3, 1, 4).reshape(2, 4, ROWS, HEAD)
    heads = dt_bias.shape[1]
    par = jnp.broadcast_to(
        jnp.concatenate([dt_bias, decay_rate], axis=0)[:, :, None], (2, heads, span)
    )
    lane_rows = jnp.concatenate(
        [jnp.repeat(skip_gain, SHEAD, axis=1), out_gain.reshape(1, heads * SHEAD)], axis=0
    )
    any_spec = pl.BlockSpec(memory_space=pl.ANY)
    vmem_spec = pl.BlockSpec(memory_space=pltpu.VMEM)
    dma = pltpu.SemaphoreType.DMA
    vm = pltpu.VMEM
    out = pl.pallas_call(
        functools.partial(kernel, nz),
        out_shape=jax.ShapeDtypeStruct(layer_in.shape, BF16),
        in_specs=[any_spec] * 5 + [vmem_spec] * 2,
        out_specs=vmem_spec,
        scratch_shapes=[
            vm((QH, span, HEAD), BF16),
            vm((nz, 4, span, HEAD), BF16),
            vm((nz, 2 * span, span), F32),
            vm(layer_in.shape, BF16),
            vm(w_bc.shape[1:], BF16),
            vm(w_dt.shape[1:], BF16),
            vm((span, GCOLS), BF16),
            vm((GROUPS, PACK, STATE), F32),
            vm((GROUPS, PACK, STATE), F32),
            vm((span, STATE), F32),
            vm((2, GHEADS, span), F32),
            vm((8, STATE), BF16),
            vm((2, span, STATE), BF16),
            vm((span, span), F32),
            vm((CHUNKS, STATE, CCOLS), F32),
            vm((CHUNKS, STATE, CCOLS), F32),
            vm((CHUNKS, STATE, CCOLS), F32),
            vm((span, GCOLS), F32),
            vm((span, GCOLS), BF16),
            dma((4,)),
            dma((2,)),
            dma((nctx,)),
            dma((nctx,)),
            dma((2,)),
            dma((3,)),
            dma((3,)),
            dma((CHUNKS,)),
            dma((CHUNKS,)),
            dma((CHUNKS,)),
            dma((CHUNKS,)),
        ],
        compiler_params=pltpu.CompilerParams(
            collective_id=0, has_side_effects=True, vmem_limit_bytes=52 * 1024 * 1024
        ),
    )(q, kv, layer_in, w_bc[0], w_dt[0], par, lane_rows)
    return out[None]


def solution(mesh):
    in_specs = (
        P("ctx", "tp", None),
        P("ctx", "tp", None),
        P("ctx", "tp", None),
        P("ctx", "tp"),
        P(None, "tp", None),
        P(None, "tp", None),
        P(None, "tp"),
        P(None, "tp"),
        P(None, "tp"),
        P(None, "tp", None),
    )
    out_specs = P("segment", "ctx", "tp")
    return jax.shard_map(body, mesh=mesh, in_specs=in_specs, out_specs=out_specs, check_vma=False)
```

time: 249 us -> 46.6 us (0.19)
  waiting for transfers between devices: 158 us -> 0 us
  Pallas kernels: 0 us -> 37 us
  blocking collectives: 26.1 us -> 0 us
  between operations: 15.9 us -> 0.03 us
  other arithmetic: 14.6 us -> 0.73 us
  local copies, waits for them, and re-layouts: 20.7 us -> 8.5 us
  matrix products: 11.2 us -> 0 us
    all_gather x3 -> x0, waiting for transfers between devices: 140 us -> none  [the longest x1 113 us: prefix(): gathered = jax.tree.map(lambda a: lax.all_gather(a, axis), part)]
    pallas_call x0 -> x1, Pallas kernels: none -> 37 us  [body(): pl.pallas_call(functools.partial(kernel, nz), out_shape=jax.ShapeDtypeStr...]
    unnamed x1 -> x0, blocking collectives: 16.8 us -> none
    psum x1 -> x0, waiting for transfers between devices: 15.9 us -> none  [body(): sum_bc, sum_dt, sum_sq = lax.psum((part_bc, part_dt, part_sq), 'tp')]
    dot_general x5 -> x0, matrix products: 11.2 us -> none  [the longest x1 3.92 us: body(): part_bc = jnp.dot(current, w_bc[0], preferred_element_type=jnp.float32)]
    psum x1 -> x0, blocking collectives: 9.3 us -> none  [body(): sum_bc, sum_dt, sum_sq = lax.psum((part_bc, part_dt, part_sq), 'tp')]
    add x7 -> x0, other arithmetic: 8.64 us -> none  [the longest x6 8.63 us: merge_states(): later[0][:, None, None] * earlier[1] + later[1]]
    mul x7 -> x0, local copies, waits for them, and re-layouts: 4.8 us -> none  [the longest x6 4.15 us: merge_states(): later[0][:, None, None] * earlier[1] + later[1]]
  transfers between devices with their start and end apart: 5 -> 0, of which waited for: 4 -> 0; matrix products, arithmetic and copies ran while one was open for 11% -> 0% of each run, Pallas kernels for 0% -> 0%
where the time goes in v1:
time: 46.6 us; the launch traced here: 46.2 us
  Pallas kernels  37 us (79%)
  local copies, waits for them, and re-layouts  8.5 us (18%)
  other arithmetic  0.73 us (2%)
    pallas_call x1, Pallas kernels, body(): pl.pallas_call(functools.partial(kernel, nz), out_shape=jax.ShapeDtypeStr...  37 us
    unnamed x4, local copies, waits for them, and re-layouts  3.79 us
    another operation x2, local copies, waits for them, and re-layouts, body(): jnp.stack([keys.reshape(ROWS, 2, 2, HEAD), values.reshape(ROWS, 2, 2, HEA...  1.85 us
    transpose x1, local copies, waits for them, and re-layouts, body(): q = queries.transpose(1, 0, 2).reshape(2, QH, ROWS, HEAD)  1.18 us

profile of v1, /device:TPU:24, one launch (start us, length us, event | category | flops | bytes accessed | tf_op | source)
XLA Modules:
  0.0 46.2 jit_solution(10087278656009188108)
XLA Ops:
  0.0 0.7 %pad_maximum_fusion.2 = f32[2,32]{1,0:T(2,128)S(1)} fusion(f32[1,32]{1,0:T(1,128)} %param.17, f32[1,32]{1,0:T(1,128)} %param.16), kind=kLoop, calls=%fused_computation.2 | loop fusion | flops 64 | bytes 512 | tf_op jit(solution)/shard_map/concatenate | solution.py:472
  0.7 0.8 %reshape.17 = f32[1,2048]{1,0:T(1,128)S(1)} reshape(f32[1,32,64]{2,1,0:T(8,128)} %param.19) | data formatting | bytes 16384 | tf_op jit(solution)/shard_map/reshape | solution.py:475
  1.5 0.7 %broadcast_in_dim.15 = f32[32,64]{1,0:T(8,128)S(1)} broadcast(f32[32]{0:T(128)} %bitcast.19), dimensions={0} | broadcast | bytes 8320 | tf_op jit(solution)/shard_map/broadcast_in_dim | solution.py:475
  2.2 0.1 broadcast_in_dim.16
  2.3 0.1 broadcast_in_dim.14.par_ref
  2.4 0.9 %copy.12 = bf16[1,128,2,2,128]{4,1,3,0,2:T(8,128)(2,1)S(1)} copy(bf16[1,128,2,2,128]{4,3,2,1,0:T(2,128)(2,1)} %bitcast.17) | data formatting | bytes 262144 | tf_op jit(solution)/shard_map/stack;reshape | solution.py:468
  3.3 0.9 %copy.13 = bf16[1,128,2,2,128]{4,1,3,0,2:T(8,128)(2,1)S(1)} copy(bf16[1,128,2,2,128]{4,3,2,1,0:T(2,128)(2,1)} %bitcast.18) | data formatting | bytes 262144 | tf_op jit(solution)/shard_map/stack;reshape | solution.py:468
  4.3 1.2 %copy.11 = bf16[16,128,128]{2,1,0:T(8,128)(2,1)S(1)} copy(bf16[16,128,128]{2,0,1:T(8,128)(2,1)} %bitcast.16) | data formatting | bytes 1048576 | tf_op jit(solution)/shard_map/transpose | solution.py:467
  5.5 2.0 %copy.14 = bf16[1,2048,64]{2,1,0:T(8,128)(2,1)} copy(bf16[1,2048,64]{1,2,0:T(8,128)(2,1)} %param.15) | data formatting | bytes 524288 | tf_op args[5]
  7.4 0.0 copy-start
  7.4 1.0 %copy-done = bf16[128,2048]{1,0:T(8,128)(2,1)S(1)} copy-done((bf16[128,2048]{1,0:T(8,128)(2,1)S(1)}, bf16[128,2048]{1,0:T(8,128)(2,1)}, u32[]{:S(2)}) %copy-start) | copy-done | bytes 524312
  8.5 37.0 %shard_map.103 = bf16[128,2048]{1,0:T(8,128)(2,1)S(1)} custom-call(bf16[2,8,128,128]{3,2,1,0:T(8,128)(2,1)S(1)} %bitcast.12, bf16[2,4,128,128]{3,2,1,0:T(8,128)(2,1)S(1)} %bitcast.13, bf16[128,2048]{1,0:T(8,128)(2,1)S(1)} %copy-done, bf16[2048,1024]{1,0:T(8,128)(2,1)} %bitcast.14, bf16[2048,64]{1,0:T(8,128)(2,1)} %bitcast.15, ...), custom_call_target="tpu_custom_call" | custom-call | tf_op jit(solution)/shard_map/pallas_call | solution.py:481
  45.4 0.8 %copy.16 = bf16[1,128,2048]{2,1,0:T(8,128)(2,1)} copy(bf16[1,128,2048]{2,1,0:T(8,128)(2,1)S(1)} %bitcast.11) | data formatting | bytes 1048576
  (2 shorter events, 0.0 us)
Async XLA Ops:
  7.4 1.0 %copy-start = (bf16[128,2048]{1,0:T(8,128)(2,1)S(1)}, bf16[128,2048]{1,0:T(8,128)(2,1)}, u32[]{:S(2)}) copy-start(bf16[128,2048]{1,0:T(8,128)(2,1)} %x_hbm.1) | copy-start | bytes 1572868

commit v2 on v1

v2 whole, which is shorter than its diff:
```python
import functools
import math

import jax
import jax.numpy as jnp
from jax import lax
from jax.experimental import pallas as pl
from jax.experimental.pallas import tpu as pltpu
from jax.sharding import PartitionSpec as P

MESH = pl.DeviceIdType.MESH
EPSILON = 1e-05
F32 = jnp.float32
BF16 = jnp.bfloat16

ROWS = 128
HEAD = 128
STATE = 128
SHEAD = 64
GHEADS = 16
GCOLS = GHEADS * SHEAD
GROUPS = 4
QH = 8
CHUNKS = 8
CCOLS = GCOLS // CHUNKS
MISC = 24
PACK = 2 * ROWS + MISC


def split(a):
    hi = a.astype(BF16)
    return hi, (a - hi.astype(F32)).astype(BF16)


def dot(a, b):
    return jnp.dot(a, b, preferred_element_type=F32)


def dot_t(a, b):
    return lax.dot_general(a, b, (((1,), (1,)), ((), ())), preferred_element_type=F32)


def dot3(a, b):
    return dot(a[0], b[0]) + (dot(a[0], b[1]) + dot(a[1], b[0]))


def dot3_t(a, b):
    return dot_t(a[0], b[0]) + (dot_t(a[0], b[1]) + dot_t(a[1], b[0]))


def lane_pair(left, right, shape):
    lane = lax.broadcasted_iota(jnp.int32, shape, 1)
    return jnp.where(lane < SHEAD, jnp.broadcast_to(left, shape), jnp.broadcast_to(right, shape))


def head_column(ref, half):
    shape = (GHEADS, ref.shape[1])
    wanted = lax.broadcasted_iota(jnp.int32, shape, 1) == (
        lax.broadcasted_iota(jnp.int32, shape, 0) + half * GHEADS
    )
    return jnp.sum(
        jnp.where(wanted, jnp.broadcast_to(ref[...], shape), 0.0), axis=1, keepdims=True
    )


def channel_rows(skip_ref, gain_ref, half):
    shape = (GHEADS, GCOLS)
    own = (
        lax.broadcasted_iota(jnp.int32, shape, 1) // SHEAD
        == lax.broadcasted_iota(jnp.int32, shape, 0)
    )
    skip = jnp.broadcast_to(head_column(skip_ref, half), shape)
    skip = jnp.sum(jnp.where(own, skip, 0.0), axis=0, keepdims=True)
    gain = gain_ref[pl.ds(pl.multiple_of(half * GHEADS, GHEADS), GHEADS), :]
    pairs = jnp.concatenate([gain, gain], axis=1)
    gain = jnp.concatenate([pairs] * (GHEADS // 2), axis=1)
    gain = jnp.sum(jnp.where(own, gain, 0.0), axis=0, keepdims=True)
    return skip, gain


def kernel(
    nz,
    q_hbm,
    k_hbm,
    v_hbm,
    x_hbm,
    w_hbm,
    wdt_hbm,
    bias_ref,
    rate_ref,
    skip_ref,
    gain_ref,
    out_ref,
    q_in,
    k_in,
    v_in,
    q_own,
    kv_own,
    qbuf,
    kvbuf,
    scores,
    xv,
    wv,
    wdtv,
    xg,
    psend,
    psend_dt,
    pbuf,
    tcols,
    rows_s,
    bt_s,
    c_s,
    cb_s,
    ending,
    s_in,
    s_out,
    local,
    stage,
    loc_sem,
    w_sem,
    q_sem,
    pkv_sem,
    kv_send,
    kv_recv,
    x_sem,
    p_send,
    p_recv,
    st_send,
    st_recv,
    o_send,
    o_recv,
):
    seg = lax.axis_index("segment")
    ctx = lax.axis_index("ctx")
    tp = lax.axis_index("tp")
    z = ctx // 2
    half = ctx % 2
    other = 1 - half
    pair = z * 2 + other
    barrier = pltpu.get_barrier_semaphore()
    my_rows = pl.ds(pl.multiple_of(half * ROWS, ROWS), ROWS)
    other_rows = pl.ds(pl.multiple_of(other * ROWS, ROWS), ROWS)
    my_cols = pl.ds(pl.multiple_of(half * GCOLS, GCOLS), GCOLS)
    other_cols = pl.ds(pl.multiple_of(other * GCOLS, GCOLS), GCOLS)

    def signal(s, c, t):
        pl.semaphore_signal(barrier, inc=1, device_id=(s, c, t), device_id_type=MESH)

    def remote(src, dst, send, recv, c, t):
        return pltpu.make_async_remote_copy(
            src_ref=src,
            dst_ref=dst,
            send_sem=send,
            recv_sem=recv,
            device_id=(seg, c, t),
            device_id_type=MESH,
        )

    @pl.when(seg == 1)
    def _attention():
        get_k = pltpu.make_async_copy(k_hbm, k_in, loc_sem.at[0])
        get_v = pltpu.make_async_copy(v_hbm, v_in, loc_sem.at[1])
        get_q = pltpu.make_async_copy(q_hbm, q_in, loc_sem.at[2])
        get_k.start()
        get_v.start()
        get_q.start()
        signal(1, pair, tp)

        @pl.when(z > 0)
        def _():
            signal(1, ctx - 2, tp)

        get_k.wait()
        get_v.wait()
        k_heads = jnp.swapaxes(k_in[...].astype(F32), 0, 1).astype(BF16)
        v_heads = jnp.swapaxes(v_in[...].astype(F32), 0, 1).astype(BF16)
        for p in range(2):
            kv_own[p, 0:2] = k_heads[2 * p : 2 * p + 2]
            kv_own[p, 2:4] = v_heads[2 * p : 2 * p + 2]
        pl.semaphore_wait(barrier, 1 + jnp.where(z < nz - 1, 1, 0))
        following = lax.rem(ctx + 2, 2 * nz)

        def pair_copy(dst_rows):
            return remote(
                kv_own.at[other], kvbuf.at[z, :, dst_rows, :], pkv_sem.at[0], pkv_sem.at[1], pair, tp
            )

        def pass_on(zz):
            return remote(
                kvbuf.at[zz], kvbuf.at[zz], kv_send.at[zz], kv_recv.at[zz], following, tp
            )

        def q_copy(dst_rows):
            return remote(
                q_own.at[other], qbuf.at[:, dst_rows, :], q_sem.at[0], q_sem.at[1], pair, tp
            )

        pair_copy(my_rows).start()
        kvbuf[z, :, my_rows, :] = kv_own[half]
        get_q.wait()
        q_own[...] = (
            jnp.swapaxes(q_in[...].astype(F32), 0, 1).astype(BF16).reshape(2, QH, ROWS, HEAD)
        )
        qbuf[:, my_rows, :] = q_own[half]
        pair_copy(other_rows).wait_recv()

        @pl.when(z < nz - 1)
        def _():
            pass_on(z).start()

        q_copy(my_rows).start()

        def arrive(k, carry):
            zz = z - 1 - k
            pass_on(zz).wait_recv()

            @pl.when(z < nz - 1)
            def _():
                pass_on(zz).start()

            return carry

        lax.fori_loop(0, z, arrive, 0)
        q_copy(other_rows).wait_recv()
        scale = 1.0 / math.sqrt(HEAD)
        span = 2 * ROWS
        rows2 = 2 * span
        t_at = lax.broadcasted_iota(jnp.int32, (rows2, span), 0) % span
        s_at = lax.broadcasted_iota(jnp.int32, (rows2, span), 1)
        allowed = t_at >= s_at

        def two_heads(i, carry):
            kvh = i // 2
            q = qbuf[pl.ds(i * 2, 2)].reshape(rows2, HEAD)
            diag = dot_t(q, kvbuf[z, kvh]) * scale
            diag = jnp.where(allowed, diag, -1e30)

            def first(zz, top):
                s = dot_t(q, kvbuf[zz, kvh]) * scale
                scores[zz] = s
                return jnp.maximum(top, jnp.max(s, axis=1, keepdims=True))

            top = lax.fori_loop(0, z, first, jnp.max(diag, axis=1, keepdims=True))
            weight = jnp.exp(diag - top)
            total = jnp.sum(weight, axis=1, keepdims=True)
            acc = dot(weight.astype(BF16), kvbuf[z, kvh + 2])

            def second(zz, kept):
                total, acc = kept
                weight = jnp.exp(scores[zz] - top)
                return (
                    total + jnp.sum(weight, axis=1, keepdims=True),
                    acc + dot(weight.astype(BF16), kvbuf[zz, kvh + 2]),
                )

            total, acc = lax.fori_loop(0, z, second, (total, acc))
            done = (acc / total).astype(BF16)
            for k in range(2):
                cols = pl.ds(pl.multiple_of((i * 2 + k) * HEAD, HEAD), HEAD)
                stage[:, cols] = done[k * span : (k + 1) * span]
            at = pl.ds(pl.multiple_of(i * 2 * HEAD, 2 * HEAD), 2 * HEAD)
            to = pl.ds(pl.multiple_of(half * GCOLS + i * 2 * HEAD, 2 * HEAD), 2 * HEAD)
            out_copy(i, half).start()
            out_ref[:, to] = stage[my_rows, at]
            return carry

        def out_copy(i, base):
            at = pl.ds(pl.multiple_of(i * 2 * HEAD, 2 * HEAD), 2 * HEAD)
            to = pl.ds(pl.multiple_of(base * GCOLS + i * 2 * HEAD, 2 * HEAD), 2 * HEAD)
            return remote(
                stage.at[other_rows, at], out_ref.at[:, to], o_send.at[i], o_recv.at[i], pair, tp
            )

        lax.fori_loop(0, QH // 2, two_heads, 0)
        for i in range(QH // 2):
            out_copy(i, half).wait_send()
            out_copy(i, other).wait_recv()

        @pl.when(z < nz - 1)
        def _():
            def sent(zz, carry):
                pass_on(zz).wait_send()
                return carry

            lax.fori_loop(0, z + 1, sent, 0)

        pair_copy(my_rows).wait_send()
        q_copy(my_rows).wait_send()

    @pl.when(seg == 0)
    def _state():
        me4 = tp * 2 + half
        get_x = pltpu.make_async_copy(x_hbm, xv, loc_sem.at[1])
        get_dt = pltpu.make_async_copy(wdt_hbm, wdtv, loc_sem.at[2])
        get_g = pltpu.make_async_copy(x_hbm.at[:, my_cols], xg.at[my_rows, :], loc_sem.at[3])
        quad = ((pair, 1 - tp), (z * 2 + half, 1 - tp), (pair, tp))
        groups = [t * 2 + c % 2 for c, t in quad] + [me4]

        def get_w(k, part):
            src = pl.ds(pl.multiple_of((part * GROUPS + groups[k]) * STATE, STATE), STATE)
            return pltpu.make_async_copy(
                w_hbm.at[:, src], wv.at[k, :, pl.ds(part * STATE, STATE)], w_sem.at[2 * k + part]
            )

        get_x.start()
        get_dt.start()
        for k in range(GROUPS):
            for part in range(2):
                get_w(k, part).start()
        get_g.start()
        for c, t in quad:
            signal(0, c, t)

        @pl.when(z > 0)
        def _():
            signal(0, ctx - 2, tp)

        more = jnp.where(z < nz - 1, 1, 0)
        pl.semaphore_wait(barrier, 3 + more)

        def x_copy(dst_rows):
            return remote(
                x_hbm.at[:, other_cols], xg.at[dst_rows, :], x_sem.at[0], x_sem.at[1], pair, tp
            )

        x_copy(my_rows).start()
        get_x.wait()
        get_dt.wait()
        x = xv[...]
        dt_all = dot_t(wdtv[...], x)
        psend_dt[...] = dt_all
        wide = x.astype(F32)
        sq_col = jnp.sum(wide * wide, axis=1, keepdims=True)
        sq_row = jnp.transpose(jnp.broadcast_to(sq_col, (ROWS, ROWS)))[0:8]

        def p_copy(k, slot):
            c, t = quad[k]
            return remote(psend.at[k], pbuf.at[slot], p_send.at[k], p_recv.at[k], c, t)

        for k in range(GROUPS):
            get_w(k, 0).wait()
            get_w(k, 1).wait()
            proj = dot(x, wv[k])
            dt_rows = pl.ds(pl.multiple_of(groups[k] * GHEADS, GHEADS), GHEADS)
            if k < 3:
                into = psend.at[k]
            else:
                into = pbuf.at[me4]
            into[0:ROWS] = proj[:, 0:STATE]
            into[ROWS : 2 * ROWS] = proj[:, STATE:]
            into[2 * ROWS : 2 * ROWS + GHEADS] = psend_dt[dt_rows]
            into[2 * ROWS + GHEADS : PACK] = sq_row
            if k < 3:
                p_copy(k, me4).start()
        for k in range(3):
            p_copy(k, groups[k]).wait_recv()

        span = 2 * ROWS
        r0 = pbuf[0] + pbuf[2]
        r1 = pbuf[1] + pbuf[3]
        b = jnp.concatenate([r0[0:ROWS], r1[0:ROWS]], axis=0)
        c_raw = jnp.concatenate([r0[ROWS : 2 * ROWS], r1[ROWS : 2 * ROWS]], axis=0)
        misc = jnp.concatenate([r0[2 * ROWS :], r1[2 * ROWS :]], axis=1)
        channels = 4 * GCOLS
        inv8 = lax.rsqrt(misc[GHEADS:MISC] / channels + EPSILON)
        inv = inv8[0:1]
        bias = head_column(bias_ref, half)
        rate = head_column(rate_ref, half)
        pre = misc[0:GHEADS] * inv + bias
        step = jnp.maximum(pre, 0.0) + jnp.log1p(jnp.exp(-jnp.abs(pre)))
        neg = -(step * rate)
        upto = (
            lax.broadcasted_iota(jnp.int32, (span, span), 0)
            <= lax.broadcasted_iota(jnp.int32, (span, span), 1)
        ).astype(F32).astype(BF16)
        n0 = neg.astype(BF16)
        rest = neg - n0.astype(F32)
        n1 = rest.astype(BF16)
        n2 = (rest - n1.astype(F32)).astype(BF16)
        log_decay = dot(n0, upto) + (dot(n1, upto) + dot(n2, upto))
        log_end = log_decay[:, span - 1 : span]
        u = step * inv
        root = math.sqrt(STATE)
        tall = jnp.concatenate(
            [
                log_decay,
                jnp.exp(log_end - log_decay) * u * inv,
                jnp.exp(log_decay) * inv / root,
                inv8,
                jnp.zeros((STATE - 3 * GHEADS - 8, span), F32),
            ],
            axis=0,
        )
        cols = jnp.transpose(tall)
        tcols[...] = cols
        rows_s[0] = log_decay
        rows_s[1] = u
        inv_col = cols[:, 3 * GHEADS : 3 * GHEADS + 1]
        bt_hi, bt_lo = split(jnp.transpose(b))
        c_hi, c_lo = split(c_raw)
        c_s[0] = c_hi
        c_s[1] = c_lo
        def columns(base, j):
            h = base + 2 * j
            return lane_pair(cols[:, h : h + 1], cols[:, h + 1 : h + 2], (span, 2 * SHEAD))

        def state_copy(j):
            return remote(
                s_out.at[j], s_in.at[j], st_send.at[j], st_recv.at[j],
                lax.rem(ctx + 2, 2 * nz), tp,
            )

        get_g.wait()
        x_copy(other_rows).wait_recv()
        for j in range(CHUNKS):
            xc = xg[:, j * CCOLS : (j + 1) * CCOLS].astype(F32)
            e = dot3((bt_hi, bt_lo), split(xc * columns(GHEADS, j)))
            ending[j] = e

            @pl.when(z == 0)
            def _():
                s_out[j] = e
                s_in[j] = jnp.zeros_like(e)
                state_copy(j).start()

        cb = dot3((c_hi, c_lo), (bt_hi, bt_lo)) * inv_col * inv / root
        lower = (
            lax.broadcasted_iota(jnp.int32, (span, span), 0)
            >= lax.broadcasted_iota(jnp.int32, (span, span), 1)
        )
        cb_s[...] = jnp.where(lower, cb, 0.0)

        last = cols[span - 8 : span][7:8]

        def pass_state(j):
            state_copy(j).wait_recv()

            @pl.when(z < nz - 1)
            def _():
                h = 2 * j
                fade = lane_pair(
                    jnp.exp(last[:, h : h + 1]), jnp.exp(last[:, h + 1 : h + 2]), (1, 2 * SHEAD)
                )
                s_out[j] = s_in[j] * fade + ending[j]
                state_copy(j).start()

        for j in range(CHUNKS):
            h = 2 * j
            xp = xg[:, h * SHEAD : (h + 2) * SHEAD]
            halves = []
            for d in range(2):
                lrow = rows_s[0, h + d : h + d + 1]
                urow = rows_s[1, h + d : h + d + 1]
                lcol = tcols[:, h + d : h + d + 1]
                top = (
                    jnp.exp(jnp.minimum(lcol[:ROWS] - lrow[:, :ROWS], 0.0))
                    * cb_s[:ROWS, :ROWS]
                    * urow[:, :ROWS]
                )
                low = jnp.exp(jnp.minimum(lcol[ROWS:] - lrow, 0.0)) * cb_s[ROWS:] * urow
                t_hi, t_lo = split(top)
                l_hi, l_lo = split(low)
                halves.append(
                    (
                        dot(t_hi, xp[:ROWS]) + dot(t_lo, xp[:ROWS]),
                        dot(l_hi, xp) + dot(l_lo, xp),
                    )
                )
            lane = lax.broadcasted_iota(jnp.int32, (ROWS, 2 * SHEAD), 1)
            at = slice(h * SHEAD, (h + 2) * SHEAD)
            local[0:ROWS, at] = jnp.where(lane < SHEAD, halves[0][0], halves[1][0])
            local[ROWS:span, at] = jnp.where(lane < SHEAD, halves[0][1], halves[1][1])

            @pl.when(z == 1)
            def _():
                pass_state(j)

        block = (
            lax.broadcasted_iota(jnp.int32, (CCOLS, CCOLS), 0) // SHEAD
            == lax.broadcasted_iota(jnp.int32, (CCOLS, CCOLS), 1) // SHEAD
        ).astype(F32).astype(BF16)

        def out_copy(j, base):
            at = pl.ds(pl.multiple_of(base * GCOLS + j * CCOLS, CCOLS), CCOLS)
            return remote(
                stage.at[other_rows, pl.ds(j * CCOLS, CCOLS)],
                out_ref.at[:, at],
                o_send.at[j],
                o_recv.at[j],
                pair,
                tp,
            )

        skip_row, gain_row = channel_rows(skip_ref, gain_ref, half)

        for j in range(CHUNKS):
            @pl.when(z > 1)
            def _():
                pass_state(j)

            at = slice(j * CCOLS, (j + 1) * CCOLS)
            xc = xg[:, at].astype(F32)
            inflow = dot3((c_s[0], c_s[1]), split(s_in[j]))
            gcols = pl.ds(pl.multiple_of(half * GCOLS + j * CCOLS, CCOLS), CCOLS)
            skip = skip_row[:, at]
            gain = gain_row[:, at]
            mixed = local[:, at] + inflow * columns(2 * GHEADS, j) + skip * (xc * inv_col)
            p_hi, p_lo = split(mixed * mixed)
            power = (dot(p_hi, block) + dot(p_lo, block)) / SHEAD
            stage[:, at] = (xc + gain * mixed * lax.rsqrt(power + EPSILON)).astype(BF16)
            out_copy(j, half).start()
            out_ref[:, gcols] = stage[my_rows, at]

        for j in range(CHUNKS):
            out_copy(j, half).wait_send()
            out_copy(j, other).wait_recv()

            @pl.when(z < nz - 1)
            def _():
                state_copy(j).wait_send()

        for k in range(3):
            p_copy(k, me4).wait_send()
        x_copy(my_rows).wait_send()


def body(queries, keys, values, layer_in, w_bc, w_dt, dt_bias, decay_rate, skip_gain, out_gain):
    nctx = lax.axis_size("ctx")
    nz = nctx // 2
    span = 2 * ROWS
    hbm_spec = pl.BlockSpec(memory_space=pltpu.HBM)
    vmem_spec = pl.BlockSpec(memory_space=pltpu.VMEM)
    dma = pltpu.SemaphoreType.DMA
    vm = pltpu.VMEM
    out = pl.pallas_call(
        functools.partial(kernel, nz),
        out_shape=jax.ShapeDtypeStruct(layer_in.shape, BF16),
        in_specs=[hbm_spec] * 6 + [vmem_spec] * 4,
        out_specs=vmem_spec,
        scratch_shapes=[
            vm(queries.shape, BF16),
            vm(keys.shape, BF16),
            vm(values.shape, BF16),
            vm((2, QH, ROWS, HEAD), BF16),
            vm((2, 4, ROWS, HEAD), BF16),
            vm((QH, span, HEAD), BF16),
            vm((nz, 4, span, HEAD), BF16),
            vm((nz, 2 * span, span), F32),
            vm(layer_in.shape, BF16),
            vm((GROUPS, w_bc.shape[1], 2 * STATE), BF16),
            vm((w_dt.shape[2], w_dt.shape[1]), BF16),
            vm((span, GCOLS), BF16),
            vm((GROUPS - 1, PACK, STATE), F32),
            vm((GROUPS * GHEADS, ROWS), F32),
            vm((GROUPS, PACK, STATE), F32),
            vm((span, STATE), F32),
            vm((2, GHEADS, span), F32),
            vm((8, STATE), BF16),
            vm((2, span, STATE), BF16),
            vm((span, span), F32),
            vm((CHUNKS, STATE, CCOLS), F32),
            vm((CHUNKS, STATE, CCOLS), F32),
            vm((CHUNKS, STATE, CCOLS), F32),
            vm((span, GCOLS), F32),
            vm((span, GCOLS), BF16),
            dma((4,)),
            dma((2 * GROUPS,)),
            dma((2,)),
            dma((2,)),
            dma((nz,)),
            dma((nz,)),
            dma((2,)),
            dma((3,)),
            dma((3,)),
            dma((CHUNKS,)),
            dma((CHUNKS,)),
            dma((CHUNKS,)),
            dma((CHUNKS,)),
        ],
        compiler_params=pltpu.CompilerParams(
            collective_id=0, has_side_effects=True, vmem_limit_bytes=60 * 1024 * 1024
        ),
    )(
        queries,
        keys,
        values,
        layer_in,
        w_bc[0],
        w_dt[0].T,
        dt_bias,
        decay_rate,
        skip_gain,
        out_gain[0],
    )
    return out[None]


def solution(mesh):
    in_specs = (
        P("ctx", "tp", None),
        P("ctx", "tp", None),
        P("ctx", "tp", None),
        P("ctx", "tp"),
        P(None, "tp", None),
        P(None, "tp", None),
        P(None, "tp"),
        P(None, "tp"),
        P(None, "tp"),
        P(None, "tp", None),
    )
    out_specs = P("segment", "ctx", "tp")
    return jax.shard_map(body, mesh=mesh, in_specs=in_specs, out_specs=out_specs, check_vma=False)
```

time: 46.6 us -> 36 us (0.77)
  local copies, waits for them, and re-layouts: 8.5 us -> 1.88 us
  Pallas kernels: 37 us -> 33.9 us
  other arithmetic: 0.73 us -> 0 us
    pallas_call x1, Pallas kernels: 37 us -> 33.9 us  [body(): pl.pallas_call(functools.partial(kernel, nz), out_shape=jax.ShapeDtypeStr...]
    unnamed x4 -> x1, local copies, waits for them, and re-layouts: 3.79 us -> 1.88 us
    another operation x2 -> x0, local copies, waits for them, and re-layouts: 1.85 us -> none  [body(): jnp.stack([keys.reshape(ROWS, 2, 2, HEAD), values.reshape(ROWS, 2, 2, HEA...]
    transpose x1 -> x0, local copies, waits for them, and re-layouts: 1.18 us -> none  [body(): q = queries.transpose(1, 0, 2).reshape(2, QH, ROWS, HEAD)]
    broadcast_in_dim x3 -> x0, local copies, waits for them, and re-layouts: 0.88 us -> none  [the longest x2 0.81 us: body(): jnp.repeat(skip_gain, SHEAD, axis=1)]
    reshape x1 -> x0, local copies, waits for them, and re-layouts: 0.8 us -> none  [body(): out_gain.reshape(1, heads * SHEAD)]
    concatenate x2 -> x0, other arithmetic: 0.7 us -> none  [the longest x1 0.68 us: body(): jnp.concatenate([dt_bias, decay_rate], axis=0)[:, :, None]]
where the time goes in v2:
time: 36 us; the launch traced here: 35.8 us
  Pallas kernels  33.9 us (94%)
  local copies, waits for them, and re-layouts  1.88 us (5%)
    pallas_call x1, Pallas kernels, body(): pl.pallas_call(functools.partial(kernel, nz), out_shape=jax.ShapeDtypeStr...  33.9 us
    unnamed x1, local copies, waits for them, and re-layouts  1.88 us

profile of v2, /device:TPU:24, one launch (start us, length us, event | category | flops | bytes accessed | tf_op | source)
XLA Modules:
  0.0 35.8 jit_solution(9100801857895890636)
XLA Ops:
  0.0 33.9 %shard_map.100 = bf16[128,2048]{1,0:T(8,128)(2,1)} custom-call(bf16[128,16,128]{2,1,0:T(8,128)(2,1)} %q_hbm.1, bf16[128,4,128]{2,1,0:T(4,128)(2,1)} %k_hbm.1, bf16[128,4,128]{2,1,0:T(4,128)(2,1)} %v_hbm.1, bf16[128,2048]{1,0:T(8,128)(2,1)} %x_hbm.1, bf16[2048,1024]{1,0:T(8,128)(2,1)} %bitcast.6, bf16[64,2048]{1,0:T(8,128)(2,1)} %bitcast.8, ...), custom_call_target="tpu_custom_call" | custom-call | tf_op jit(solution)/shard_map/pallas_call | solution.py:535
  33.9 1.9 %copy.12 = bf16[1,128,2048]{2,1,0:T(8,128)(2,1)} copy(bf16[1,128,2048]{2,1,0:T(8,128)(2,1)} %bitcast.7) | data formatting | bytes 1048576

commit v3 on v2

--- a/solution.py
+++ b/solution.py
@@ -117,7 +117,6 @@
     local,
     stage,
     loc_sem,
-    w_sem,
     q_sem,
     pkv_sem,
     kv_send,
@@ -185,10 +184,10 @@
                 kv_own.at[other], kvbuf.at[z, :, dst_rows, :], pkv_sem.at[0], pkv_sem.at[1], pair, tp
             )
 
-        def pass_on(zz):
-            return remote(
-                kvbuf.at[zz], kvbuf.at[zz], kv_send.at[zz], kv_recv.at[zz], following, tp
-            )
+        def pass_on(zz, part):
+            block = kvbuf.at[zz, pl.ds(2 * part, 2)]
+            at = 2 * zz + part
+            return remote(block, block, kv_send.at[at], kv_recv.at[at], following, tp)
 
         def q_copy(dst_rows):
             return remote(
@@ -206,17 +205,19 @@
 
         @pl.when(z < nz - 1)
         def _():
-            pass_on(z).start()
+            pass_on(z, 0).start()
+            pass_on(z, 1).start()
 
         q_copy(my_rows).start()
 
         def arrive(k, carry):
             zz = z - 1 - k
-            pass_on(zz).wait_recv()
-
-            @pl.when(z < nz - 1)
-            def _():
-                pass_on(zz).start()
+            for part in range(2):
+                pass_on(zz, part).wait_recv()
+
+                @pl.when(z < nz - 1)
+                def _():
+                    pass_on(zz, part).start()
 
             return carry
 
@@ -279,7 +280,8 @@
         @pl.when(z < nz - 1)
         def _():
             def sent(zz, carry):
-                pass_on(zz).wait_send()
+                pass_on(zz, 0).wait_send()
+                pass_on(zz, 1).wait_send()
                 return carry
 
             lax.fori_loop(0, z + 1, sent, 0)
@@ -296,17 +298,10 @@
         quad = ((pair, 1 - tp), (z * 2 + half, 1 - tp), (pair, tp))
         groups = [t * 2 + c % 2 for c, t in quad] + [me4]
 
-        def get_w(k, part):
-            src = pl.ds(pl.multiple_of((part * GROUPS + groups[k]) * STATE, STATE), STATE)
-            return pltpu.make_async_copy(
-                w_hbm.at[:, src], wv.at[k, :, pl.ds(part * STATE, STATE)], w_sem.at[2 * k + part]
-            )
-
+        get_w = pltpu.make_async_copy(w_hbm, wv, loc_sem.at[0])
+        get_w.start()
         get_x.start()
         get_dt.start()
-        for k in range(GROUPS):
-            for part in range(2):
-                get_w(k, part).start()
         get_g.start()
         for c, t in quad:
             signal(0, c, t)
@@ -323,7 +318,6 @@
                 x_hbm.at[:, other_cols], xg.at[dst_rows, :], x_sem.at[0], x_sem.at[1], pair, tp
             )
 
-        x_copy(my_rows).start()
         get_x.wait()
         get_dt.wait()
         x = xv[...]
@@ -337,10 +331,12 @@
             c, t = quad[k]
             return remote(psend.at[k], pbuf.at[slot], p_send.at[k], p_recv.at[k], c, t)
 
+        x_copy(my_rows).start()
+        get_w.wait()
         for k in range(GROUPS):
-            get_w(k, 0).wait()
-            get_w(k, 1).wait()
-            proj = dot(x, wv[k])
+            at_b = pl.ds(pl.multiple_of(groups[k] * STATE, STATE), STATE)
+            at_c = pl.ds(pl.multiple_of((GROUPS + groups[k]) * STATE, STATE), STATE)
+            proj = dot(x, jnp.concatenate([wv[:, at_b], wv[:, at_c]], axis=1))
             dt_rows = pl.ds(pl.multiple_of(groups[k] * GHEADS, GHEADS), GHEADS)
             if k < 3:
                 into = psend.at[k]
@@ -404,11 +400,13 @@
             h = base + 2 * j
             return lane_pair(cols[:, h : h + 1], cols[:, h + 1 : h + 2], (span, 2 * SHEAD))
 
+        following = lax.rem(ctx + 2, 2 * nz)
+
+        def first_copy(j):
+            return remote(ending.at[j], s_in.at[j], st_send.at[j], st_recv.at[j], following, tp)
+
         def state_copy(j):
-            return remote(
-                s_out.at[j], s_in.at[j], st_send.at[j], st_recv.at[j],
-                lax.rem(ctx + 2, 2 * nz), tp,
-            )
+            return remote(s_out.at[j], s_in.at[j], st_send.at[j], st_recv.at[j], following, tp)
 
         get_g.wait()
         x_copy(other_rows).wait_recv()
@@ -417,11 +415,14 @@
             e = dot3((bt_hi, bt_lo), split(xc * columns(GHEADS, j)))
             ending[j] = e
 
-            @pl.when(z == 0)
-            def _():
-                s_out[j] = e
-                s_in[j] = jnp.zeros_like(e)
-                state_copy(j).start()
+        @pl.when(z == 0)
+        def _():
+            for j in range(CHUNKS):
+                first_copy(j).start()
+
+        @pl.when(z == 0)
+        def _():
+            s_in[...] = jnp.zeros_like(s_in)
 
         cb = dot3((c_hi, c_lo), (bt_hi, bt_lo)) * inv_col * inv / root
         lower = (
@@ -431,6 +432,7 @@
         cb_s[...] = jnp.where(lower, cb, 0.0)
 
         last = cols[span - 8 : span][7:8]
+        skip_row, gain_row = channel_rows(skip_ref, gain_ref, half)
 
         def pass_state(j):
             state_copy(j).wait_recv()
@@ -471,52 +473,61 @@
             local[0:ROWS, at] = jnp.where(lane < SHEAD, halves[0][0], halves[1][0])
             local[ROWS:span, at] = jnp.where(lane < SHEAD, halves[0][1], halves[1][1])
 
-            @pl.when(z == 1)
-            def _():
-                pass_state(j)
+            if j % 2 == 1:
+
+                @pl.when(z == 1)
+                def _():
+                    pass_state(j - 1)
+                    pass_state(j)
 
         block = (
             lax.broadcasted_iota(jnp.int32, (CCOLS, CCOLS), 0) // SHEAD
             == lax.broadcasted_iota(jnp.int32, (CCOLS, CCOLS), 1) // SHEAD
         ).astype(F32).astype(BF16)
 
-        def out_copy(j, base):
-            at = pl.ds(pl.multiple_of(base * GCOLS + j * CCOLS, CCOLS), CCOLS)
+        def out_copy(i, base):
+            at = pl.ds(pl.multiple_of(base * GCOLS + 2 * i * CCOLS, 2 * CCOLS), 2 * CCOLS)
             return remote(
-                stage.at[other_rows, pl.ds(j * CCOLS, CCOLS)],
+                stage.at[other_rows, pl.ds(2 * i * CCOLS, 2 * CCOLS)],
                 out_ref.at[:, at],
-                o_send.at[j],
-                o_recv.at[j],
+                o_send.at[i],
+                o_recv.at[i],
                 pair,
                 tp,
             )
 
-        skip_row, gain_row = channel_rows(skip_ref, gain_ref, half)
-
         for j in range(CHUNKS):
-            @pl.when(z > 1)
-            def _():
-                pass_state(j)
+            if j % 2 == 0:
+
+                @pl.when(z > 1)
+                def _():
+                    pass_state(j)
+                    pass_state(j + 1)
 
             at = slice(j * CCOLS, (j + 1) * CCOLS)
             xc = xg[:, at].astype(F32)
             inflow = dot3((c_s[0], c_s[1]), split(s_in[j]))
-            gcols = pl.ds(pl.multiple_of(half * GCOLS + j * CCOLS, CCOLS), CCOLS)
             skip = skip_row[:, at]
             gain = gain_row[:, at]
             mixed = local[:, at] + inflow * columns(2 * GHEADS, j) + skip * (xc * inv_col)
             p_hi, p_lo = split(mixed * mixed)
             power = (dot(p_hi, block) + dot(p_lo, block)) / SHEAD
             stage[:, at] = (xc + gain * mixed * lax.rsqrt(power + EPSILON)).astype(BF16)
-            out_copy(j, half).start()
-            out_ref[:, gcols] = stage[my_rows, at]
+            if j % 2 == 1:
+                out_copy(j // 2, half).start()
+                two = slice((j - 1) * CCOLS, (j + 1) * CCOLS)
+                out_ref[:, pl.ds(pl.multiple_of(half * GCOLS + (j - 1) * CCOLS, 2 * CCOLS), 2 * CCOLS)] = (
+                    stage[my_rows, two]
+                )
 
         for j in range(CHUNKS):
-            out_copy(j, half).wait_send()
-            out_copy(j, other).wait_recv()
-
-            @pl.when(z < nz - 1)
-            def _():
+            if j % 2 == 1:
+                out_copy(j // 2, half).wait_send()
+                out_copy(j // 2, other).wait_recv()
+
+        @pl.when(z < nz - 1)
+        def _():
+            for j in range(CHUNKS):
                 state_copy(j).wait_send()
 
         for k in range(3):
@@ -547,7 +558,7 @@
             vm((nz, 4, span, HEAD), BF16),
             vm((nz, 2 * span, span), F32),
             vm(layer_in.shape, BF16),
-            vm((GROUPS, w_bc.shape[1], 2 * STATE), BF16),
+            vm(w_bc.shape[1:], BF16),
             vm((w_dt.shape[2], w_dt.shape[1]), BF16),
             vm((span, GCOLS), BF16),
             vm((GROUPS - 1, PACK, STATE), F32),
@@ -564,11 +575,10 @@
             vm((span, GCOLS), F32),
             vm((span, GCOLS), BF16),
             dma((4,)),
-            dma((2 * GROUPS,)),
             dma((2,)),
             dma((2,)),
-            dma((nz,)),
-            dma((nz,)),
+            dma((2 * nz,)),
+            dma((2 * nz,)),
             dma((2,)),
             dma((3,)),
             dma((3,)),

time: 36 us -> 37.2 us (1.033)
  Pallas kernels: 33.9 us -> 35.1 us
    pallas_call x1, Pallas kernels: 33.9 us -> 35.1 us  [body(): pl.pallas_call(functools.partial(kernel, nz), out_shape=jax.ShapeDtypeStr...]
where the time goes in v3:
time: 37.2 us; the launch traced here: 37 us
  Pallas kernels  35.1 us (94%)
  local copies, waits for them, and re-layouts  1.88 us (5%)
    pallas_call x1, Pallas kernels, body(): pl.pallas_call(functools.partial(kernel, nz), out_shape=jax.ShapeDtypeStr...  35.1 us
    unnamed x1, local copies, waits for them, and re-layouts  1.88 us

profile of v3, /device:TPU:24, one launch (start us, length us, event | category | flops | bytes accessed | tf_op | source)
XLA Modules:
  0.0 37.0 jit_solution(12626742544054389922)
XLA Ops:
  0.0 35.1 %shard_map.100 = bf16[128,2048]{1,0:T(8,128)(2,1)} custom-call(bf16[128,16,128]{2,1,0:T(8,128)(2,1)} %q_hbm.1, bf16[128,4,128]{2,1,0:T(4,128)(2,1)} %k_hbm.1, bf16[128,4,128]{2,1,0:T(4,128)(2,1)} %v_hbm.1, bf16[128,2048]{1,0:T(8,128)(2,1)} %x_hbm.1, bf16[2048,1024]{1,0:T(8,128)(2,1)} %bitcast.6, bf16[64,2048]{1,0:T(8,128)(2,1)} %bitcast.8, ...), custom_call_target="tpu_custom_call" | custom-call | tf_op jit(solution)/shard_map/pallas_call | solution.py:546
  35.1 1.9 %copy.12 = bf16[1,128,2048]{2,1,0:T(8,128)(2,1)} copy(bf16[1,128,2048]{2,1,0:T(8,128)(2,1)} %bitcast.7) | data formatting | bytes 1048576

commit v4 on v3

--- a/solution.py
+++ b/solution.py
@@ -208,7 +208,11 @@
             pass_on(z, 0).start()
             pass_on(z, 1).start()
 
-        q_copy(my_rows).start()
+        @pl.when(z < nz - 1)
+        def _():
+            pass_on(z, 0).wait_send()
+            pass_on(z, 1).wait_send()
+            q_copy(my_rows).start()
 
         def arrive(k, carry):
             zz = z - 1 - k
@@ -218,6 +222,10 @@
                 @pl.when(z < nz - 1)
                 def _():
                     pass_on(zz, part).start()
+
+            @pl.when(jnp.logical_and(z == nz - 1, k == 0))
+            def _():
+                q_copy(my_rows).start()
 
             return carry
 
@@ -284,7 +292,7 @@
                 pass_on(zz, 1).wait_send()
                 return carry
 
-            lax.fori_loop(0, z + 1, sent, 0)
+            lax.fori_loop(0, z, sent, 0)
 
         pair_copy(my_rows).wait_send()
         q_copy(my_rows).wait_send()
@@ -318,11 +326,13 @@
                 x_hbm.at[:, other_cols], xg.at[dst_rows, :], x_sem.at[0], x_sem.at[1], pair, tp
             )
 
+        x_copy(my_rows).start()
         get_x.wait()
         get_dt.wait()
         x = xv[...]
-        dt_all = dot_t(wdtv[...], x)
-        psend_dt[...] = dt_all
+        dt_all = dot_t(x, wdtv[...])
+        dt_all = jnp.concatenate([dt_all, jnp.zeros_like(dt_all)], axis=1)
+        psend_dt[...] = jnp.transpose(dt_all)[0 : GROUPS * GHEADS]
         wide = x.astype(F32)
         sq_col = jnp.sum(wide * wide, axis=1, keepdims=True)
         sq_row = jnp.transpose(jnp.broadcast_to(sq_col, (ROWS, ROWS)))[0:8]
@@ -331,7 +341,6 @@
             c, t = quad[k]
             return remote(psend.at[k], pbuf.at[slot], p_send.at[k], p_recv.at[k], c, t)
 
-        x_copy(my_rows).start()
         get_w.wait()
         for k in range(GROUPS):
             at_b = pl.ds(pl.multiple_of(groups[k] * STATE, STATE), STATE)
@@ -400,6 +409,9 @@
             h = base + 2 * j
             return lane_pair(cols[:, h : h + 1], cols[:, h + 1 : h + 2], (span, 2 * SHEAD))
 
+        def two_columns(base, i):
+            return jnp.concatenate([columns(base, 2 * i), columns(base, 2 * i + 1)], axis=1)
+
         following = lax.rem(ctx + 2, 2 * nz)
 
         def first_copy(j):
@@ -410,15 +422,26 @@
 
         get_g.wait()
         x_copy(other_rows).wait_recv()
-        for j in range(CHUNKS):
-            xc = xg[:, j * CCOLS : (j + 1) * CCOLS].astype(F32)
-            e = dot3((bt_hi, bt_lo), split(xc * columns(GHEADS, j)))
-            ending[j] = e
+        bt_both = jnp.concatenate([bt_hi, bt_lo], axis=0)
+
+        def find_endings(send):
+            for i in range(CHUNKS // 2):
+                wide = xg[:, 2 * i * CCOLS : 2 * (i + 1) * CCOLS].astype(F32)
+                x_hi, x_lo = split(wide * two_columns(GHEADS, i))
+                both = dot(bt_both, x_hi)
+                e = both[:STATE] + (both[STATE:] + dot(bt_hi, x_lo))
+                for k in range(2):
+                    ending[2 * i + k] = e[:, k * CCOLS : (k + 1) * CCOLS]
+                    if send:
+                        first_copy(2 * i + k).start()
 
         @pl.when(z == 0)
         def _():
-            for j in range(CHUNKS):
-                first_copy(j).start()
+            find_endings(True)
+
+        @pl.when(z > 0)
+        def _():
+            find_endings(False)
 
         @pl.when(z == 0)
         def _():
@@ -436,20 +459,18 @@
 
         def pass_state(j):
             state_copy(j).wait_recv()
-
-            @pl.when(z < nz - 1)
-            def _():
-                h = 2 * j
-                fade = lane_pair(
-                    jnp.exp(last[:, h : h + 1]), jnp.exp(last[:, h + 1 : h + 2]), (1, 2 * SHEAD)
-                )
-                s_out[j] = s_in[j] * fade + ending[j]
-                state_copy(j).start()
+            h = 2 * j
+            fade = lane_pair(
+                jnp.exp(last[:, h : h + 1]), jnp.exp(last[:, h + 1 : h + 2]), (1, 2 * SHEAD)
+            )
+            s_out[j] = s_in[j] * fade + ending[j]
+            state_copy(j).start()
 
         for j in range(CHUNKS):
             h = 2 * j
             xp = xg[:, h * SHEAD : (h + 2) * SHEAD]
-            halves = []
+            tops = []
+            lows = []
             for d in range(2):
                 lrow = rows_s[0, h + d : h + d + 1]
                 urow = rows_s[1, h + d : h + d + 1]
@@ -460,29 +481,36 @@
                     * urow[:, :ROWS]
                 )
                 low = jnp.exp(jnp.minimum(lcol[ROWS:] - lrow, 0.0)) * cb_s[ROWS:] * urow
-                t_hi, t_lo = split(top)
-                l_hi, l_lo = split(low)
-                halves.append(
-                    (
-                        dot(t_hi, xp[:ROWS]) + dot(t_lo, xp[:ROWS]),
-                        dot(l_hi, xp) + dot(l_lo, xp),
-                    )
-                )
+                tops += split(top)
+                lows += split(low)
+            top = dot(jnp.concatenate(tops, axis=0), xp[:ROWS])
+            low = dot(jnp.concatenate(lows, axis=0), xp)
             lane = lax.broadcasted_iota(jnp.int32, (ROWS, 2 * SHEAD), 1)
             at = slice(h * SHEAD, (h + 2) * SHEAD)
-            local[0:ROWS, at] = jnp.where(lane < SHEAD, halves[0][0], halves[1][0])
-            local[ROWS:span, at] = jnp.where(lane < SHEAD, halves[0][1], halves[1][1])
+            for first, o in ((0, top), (ROWS, low)):
+                local[first : first + ROWS, at] = jnp.where(
+                    lane < SHEAD,
+                    o[0:ROWS] + o[ROWS : 2 * ROWS],
+                    o[2 * ROWS : 3 * ROWS] + o[3 * ROWS : 4 * ROWS],
+                )
 
             if j % 2 == 1:
 
-                @pl.when(z == 1)
+                @pl.when(jnp.logical_and(z == 1, z < nz - 1))
                 def _():
                     pass_state(j - 1)
                     pass_state(j)
 
+                if j > 1:
+
+                    @pl.when(jnp.logical_and(z > 1, z < nz - 1))
+                    def _():
+                        pass_state(j - 3)
+                        pass_state(j - 2)
+
         block = (
-            lax.broadcasted_iota(jnp.int32, (CCOLS, CCOLS), 0) // SHEAD
-            == lax.broadcasted_iota(jnp.int32, (CCOLS, CCOLS), 1) // SHEAD
+            lax.broadcasted_iota(jnp.int32, (2 * CCOLS, 2 * CCOLS), 0) // SHEAD
+            == lax.broadcasted_iota(jnp.int32, (2 * CCOLS, 2 * CCOLS), 1) // SHEAD
         ).astype(F32).astype(BF16)
 
         def out_copy(i, base):
@@ -496,29 +524,35 @@
                 tp,
             )
 
-        for j in range(CHUNKS):
-            if j % 2 == 0:
-
-                @pl.when(z > 1)
-                def _():
-                    pass_state(j)
-                    pass_state(j + 1)
-
-            at = slice(j * CCOLS, (j + 1) * CCOLS)
+        @pl.when(jnp.logical_and(z > 1, z < nz - 1))
+        def _():
+            pass_state(CHUNKS - 2)
+            pass_state(CHUNKS - 1)
+
+        c_both = c_s[...].reshape(2 * span, STATE)
+        for i in range(CHUNKS // 2):
+
+            @pl.when(jnp.logical_and(z > 0, z == nz - 1))
+            def _():
+                state_copy(2 * i).wait_recv()
+                state_copy(2 * i + 1).wait_recv()
+
+            at = slice(2 * i * CCOLS, 2 * (i + 1) * CCOLS)
             xc = xg[:, at].astype(F32)
-            inflow = dot3((c_s[0], c_s[1]), split(s_in[j]))
-            skip = skip_row[:, at]
-            gain = gain_row[:, at]
-            mixed = local[:, at] + inflow * columns(2 * GHEADS, j) + skip * (xc * inv_col)
+            s_hi, s_lo = split(jnp.concatenate([s_in[2 * i], s_in[2 * i + 1]], axis=1))
+            both = dot(c_both, s_hi)
+            inflow = both[:span] + (both[span:] + dot(c_s[0], s_lo))
+            mixed = (
+                local[:, at]
+                + inflow * two_columns(2 * GHEADS, i)
+                + skip_row[:, at] * (xc * inv_col)
+            )
             p_hi, p_lo = split(mixed * mixed)
             power = (dot(p_hi, block) + dot(p_lo, block)) / SHEAD
-            stage[:, at] = (xc + gain * mixed * lax.rsqrt(power + EPSILON)).astype(BF16)
-            if j % 2 == 1:
-                out_copy(j // 2, half).start()
-                two = slice((j - 1) * CCOLS, (j + 1) * CCOLS)
-                out_ref[:, pl.ds(pl.multiple_of(half * GCOLS + (j - 1) * CCOLS, 2 * CCOLS), 2 * CCOLS)] = (
-                    stage[my_rows, two]
-                )
+            stage[:, at] = (xc + gain_row[:, at] * mixed * lax.rsqrt(power + EPSILON)).astype(BF16)
+            out_copy(i, half).start()
+            to = pl.ds(pl.multiple_of(half * GCOLS + 2 * i * CCOLS, 2 * CCOLS), 2 * CCOLS)
+            out_ref[:, to] = stage[my_rows, at]
 
         for j in range(CHUNKS):
             if j % 2 == 1:
@@ -545,7 +579,7 @@
     vm = pltpu.VMEM
     out = pl.pallas_call(
         functools.partial(kernel, nz),
-        out_shape=jax.ShapeDtypeStruct(layer_in.shape, BF16),
+        out_shape=pltpu.VMEM(layer_in.shape, BF16),
         in_specs=[hbm_spec] * 6 + [vmem_spec] * 4,
         out_specs=vmem_spec,
         scratch_shapes=[

time: 37.2 us -> 32.3 us (0.87)
  Pallas kernels: 35.1 us -> 31.2 us
  local copies, waits for them, and re-layouts: 1.88 us -> 0.8 us
    pallas_call x1, Pallas kernels: 35.1 us -> 31.2 us  [body(): pl.pallas_call(functools.partial(kernel, nz), out_shape=pltpu.VMEM(layer_...]
    unnamed x1, local copies, waits for them, and re-layouts: 1.88 us -> 0.8 us
where the time goes in v4:
time: 32.3 us; the launch traced here: 32 us
  Pallas kernels  31.2 us (97%)
  local copies, waits for them, and re-layouts  0.8 us (2%)
    pallas_call x1, Pallas kernels, body(): pl.pallas_call(functools.partial(kernel, nz), out_shape=pltpu.VMEM(layer_...  31.2 us
    unnamed x1, local copies, waits for them, and re-layouts  0.8 us

profile of v4, /device:TPU:24, one launch (start us, length us, event | category | flops | bytes accessed | tf_op | source)
XLA Modules:
  0.0 32.0 jit_solution(7503020931052291549)
XLA Ops:
  0.0 31.2 %shard_map.100 = bf16[128,2048]{1,0:T(8,128)(2,1)S(1)} custom-call(bf16[128,16,128]{2,1,0:T(8,128)(2,1)} %q_hbm.1, bf16[128,4,128]{2,1,0:T(4,128)(2,1)} %k_hbm.1, bf16[128,4,128]{2,1,0:T(4,128)(2,1)} %v_hbm.1, bf16[128,2048]{1,0:T(8,128)(2,1)} %x_hbm.1, bf16[2048,1024]{1,0:T(8,128)(2,1)} %bitcast.7, bf16[64,2048]{1,0:T(8,128)(2,1)} %bitcast.8, ...), custom_call_target="tpu_custom_call" | custom-call | tf_op jit(solution)/shard_map/pallas_call | solution.py:580
  31.3 0.8 %copy.12 = bf16[1,128,2048]{2,1,0:T(8,128)(2,1)} copy(bf16[1,128,2048]{2,1,0:T(8,128)(2,1)S(1)} %bitcast.6) | data formatting | bytes 1048576
